TPU v7x, 256 devices: a whole 4x4x8 slice. The times are simulated.
256 devices in a mesh: dp: 32 (over y, z), tensor: 8 (over x, core).
Axes of the slice: x: 4, y: 4, z: 8, core: 2. Of those that a mesh axis runs over, the one named last changes fastest.
Arguments:
- acts: bfloat16 [32768, 5120], P('dp', 'tensor'), may hold values from -6 to 6
- out_grad: bfloat16 [32768, 2048], P(('dp', 'tensor')), may hold values from -0.1875 to 0.1875
- momentum: float32 [163840, 2048], P(('dp', 'tensor')), may hold values from -100 to 100
- q_basis: float32 [2048, 256], P('tensor'), may hold values from -0.125 to 0.125
Outputs:
- new_momentum: float32 [163840, 2048], P(('dp', 'tensor'))
- ortho: float32 [5120, 256], P('tensor')
- new_q: float32 [2048, 256], P('tensor')
All inputs are finite; a program needn't handle non-finite values.
Results may differ from a plain program's by a relative error of at most 0.0003.
Values may be sent and summed in bfloat16 or wider, within the bound.
A program may use at most 64 MiB of HBM per device.

v0:
```python
import jax
import jax.numpy as jnp
from jax import lax
from jax.sharding import Mesh
from jax.sharding import PartitionSpec as P

DP = ("dp_0", "dp_1")
TENSOR = ("tensor_0", "tensor_1")
DP_TENSOR = ("dp_0", "dp_1", "tensor_0", "tensor_1")


HIGH = lax.Precision.HIGHEST


def from_everyone(value, axis):
    copies = jnp.broadcast_to(value, (lax.axis_size(axis), *value.shape))
    return lax.all_to_all(copies, axis, split_axis=0, concat_axis=0, tiled=True)


def in_order(blocks, dim):
    blocks = jnp.moveaxis(blocks, 0, dim)
    dims = blocks.shape
    return blocks.reshape(*dims[:dim], dims[dim] * dims[dim + 1], *dims[dim + 2 :])


def whole_of(value, axes, dim):
    far, near = axes
    blocks = from_everyone(from_everyone(value, far), near)
    return in_order(blocks.swapaxes(0, 1).reshape(-1, *value.shape), dim)


def filled_up(lines, count):
    spare = -len(lines) % count
    return jnp.pad(lines, [(0, spare)] + [(0, 0)] * (lines.ndim - 1))


def collect(value, axis, dim):
    blocks = from_everyone(value, axis)
    return in_order(blocks, dim)


def split_up(value, dim, count):
    dims = value.shape
    blocks = value.reshape(*dims[:dim], count, dims[dim] // count, *dims[dim + 1 :])
    return jnp.moveaxis(blocks, dim, 0)


def summed_on_arrival(value, axis, dim):
    blocks = split_up(value, dim, lax.axis_size(axis))
    arrived = lax.all_to_all(blocks, axis, split_axis=0, concat_axis=0, tiled=True)
    return arrived.sum(axis=0)


def sum_by_parts(value, axes):
    lines = value.reshape(-1, value.shape[-1])
    padded = filled_up(lines, lax.axis_size(axes))
    whole = collect(summed_on_arrival(padded, axes, 0), axes, 0)
    return lax.slice_in_dim(whole, 0, len(lines)).reshape(value.shape)


def of_everyone(value, axis):
    return from_everyone(value, axis).sum(axis=0)


def summed_rows(value, axes, dim):
    far, near = axes
    own = summed_on_arrival(split_up(value, dim, lax.axis_size(far)), near, dim + 1)
    return jnp.sum(lax.all_to_all(own, far, 0, 0, tiled=True), axis=0)


def sum_by_parts_2(value, axes):
    lines = value.reshape(-1, value.shape[-1])
    padded = filled_up(lines, lax.axis_size(axes[0]) * lax.axis_size(axes[1]))
    whole = whole_of(summed_rows(padded, axes, 0), axes, 0)
    return lax.slice_in_dim(whole, 0, len(lines)).reshape(value.shape)


def contract_rows(first, second):
    return lax.dot_general(
        first, second, (((0,), (0,)), ((), ())), precision=HIGH, preferred_element_type=jnp.float32
    )


def orthonormal(left, gram):
    chol = jnp.linalg.cholesky(gram)
    return lax.linalg.triangular_solve(chol, left, left_side=False, lower=True, transpose_a=True)


def body(acts, out_grad, momentum, q_basis):
    width_out = out_grad.shape[1]
    replicas = lax.axis_size(DP)
    grad = lax.dot_general(
        acts,
        whole_of(out_grad, ("tensor_0", "tensor_1"), 0),
        (((0,), (0,)), ((), ())),
        preferred_element_type=jnp.float32,
    )
    buffer = 0.95 * momentum + grad
    left_local = jnp.dot(
        buffer,
        whole_of(q_basis, ("tensor_0", "tensor_1"), 0),
        precision=HIGH,
        preferred_element_type=jnp.float32,
    )
    left = sum_by_parts(left_local, DP) / replicas
    gram = of_everyone(contract_rows(left, left), TENSOR)
    ortho = orthonormal(left, gram)
    right = (
        sum_by_parts_2(contract_rows(buffer, ortho), (("dp_0", "dp_1"), ("tensor_0", "tensor_1")))
        / replicas
    )
    update = jnp.dot(ortho, right.T, precision=HIGH, preferred_element_type=jnp.float32)
    new_momentum = buffer - 0.05 * update
    own_rows = width_out // lax.axis_size(TENSOR)
    right_own = lax.dynamic_slice_in_dim(right, lax.axis_index(TENSOR) * own_rows, own_rows, 0)
    col_squares = jnp.sum(right * right, axis=0, keepdims=True)
    new_q = right_own * lax.rsqrt(col_squares + 1e-06)
    return (new_momentum, ortho, new_q)


def solution(mesh):
    split = Mesh(mesh.devices.reshape(4, 8, 4, 2), ("dp_0", "dp_1", "tensor_0", "tensor_1"))
    return jax.shard_map(
        body,
        mesh=split,
        in_specs=(P(DP, TENSOR), P(DP_TENSOR, None), P(DP_TENSOR, None), P(TENSOR, None)),
        out_specs=(P(DP_TENSOR, None), P(TENSOR, None), P(TENSOR, None)),
        check_vma=False,
    )
```

profile of v0, /device:TPU:1, one launch (start us, length us, event | category | flops | bytes accessed | tf_op | source)
XLA Modules:
  0.0 365.1 jit_solution(6392471793871680039)
XLA Ops:
  0.6 1.1 broadcast_in_dim.29
  1.8 18.8 %all_to_all.55 = f32[4,256,256]{2,1,0:T(8,128)S(1)} all-to-all(f32[4,256,256]{2,1,0:T(8,128)S(1)} %broadcast_in_dim.29), channel_id=1, replica_groups=mesh['dp_0'=4,'dp_1'=8,'tensor_0'=4,'tensor_1'=2] {'tensor_0'}, dimensions={0} | all-to-all | bytes 2097152 | tf_op jit(solution)/shard_map/all_to_all | solution.py:17
  20.7 8.0 %all_to_all.56 = f32[2,4,256,256]{3,2,1,0:T(8,128)} all-to-all(f32[2,4,256,256]{3,2,1,0:T(8,128)S(1)} %broadcast_in_dim.30), channel_id=1, replica_groups=mesh['dp_0'=4,'dp_1'=8,'tensor_0'=4,'tensor_1'=2] {'tensor_1'}, dimensions={0} | all-to-all | bytes 4194304 | tf_op jit(solution)/shard_map/all_to_all | solution.py:17
  28.7 1.6 broadcast_in_dim.27
  30.3 3.6 all-to-all-start
  33.9 3.1 copy.30
  37.0 23.0 %all-to-all-done = bf16[4,128,2048]{2,1,0:T(8,128)(2,1)S(1)} async-done(((bf16[4,128,2048]{2,1,0:T(8,128)(2,1)}), bf16[4,128,2048]{2,1,0:T(8,128)(2,1)S(1)}, u32[]{:S(2)}, u32[]{:S(2)}) %all-to-all-start) | async-done | bytes 2097184 | tf_op jit(solution)/shard_map/all_to_all | solution.py:17
  60.0 0.5 broadcast_in_dim.28
  60.5 8.2 %all_to_all.57 = bf16[2,4,128,2048]{3,2,1,0:T(8,128)(2,1)S(1)} all-to-all(bf16[2,4,128,2048]{3,2,1,0:T(8,128)(2,1)S(1)} %broadcast_in_dim.28), channel_id=1, replica_groups=mesh['dp_0'=4,'dp_1'=8,'tensor_0'=4,'tensor_1'=2] {'tensor_1'}, dimensions={0} | all-to-all | bytes 8388608 | tf_op jit(solution)/shard_map/all_to_all | solution.py:17
  68.7 0.6 copy.29
  69.3 0.6 slice-done.1
  70.0 4.7 %multiply_add_fusion = f32[640,2048]{1,0:T(8,128)} fusion(f32[640,2048]{1,0:T(8,128)S(1)} %bitcast.63, bf16[1024,640]{1,0:T(8,128)(2,1)S(1)} %copy-done, bf16[1024,2048]{1,0:T(8,128)(2,1)S(1)} %bitcast.55), kind=kOutput, calls=%fused_computation.3 | convolution fusion | flops 2686976000 | bytes 15990784 | tf_op jit(solution)/shard_map/dot_general | solution.py:92
  74.7 6.9 %dot_general.18 = f32[32,20,2048]{2,1,0:T(8,128)} reshape(f32[640,2048]{1,0:T(8,128)} %multiply_add_fusion) | data formatting | bytes 10485760 | tf_op jit(solution)/shard_map/dot_general | solution.py:99
  81.5 7.2 %fusion.10 = f32[32,20,256]{2,1,0:T(8,128)S(1)} fusion(f32[32,20,2048]{2,1,0:T(8,128)} %dot_general.18, f32[2048,256,1]{1,0,2:T(8,128)S(1)} %bitcast.60), kind=kOutput, calls=%fused_computation.39 | convolution fusion | flops 4026531840 | bytes 7995392 | tf_op jit(solution)/shard_map/dot_general | solution.py:99
  88.8 29.8 %all_to_all.58 = f32[32,20,256]{2,1,0:T(8,128)S(1)} all-to-all(f32[32,20,256]{2,1,0:T(8,128)S(1)} %fusion.10), channel_id=1, replica_groups=mesh['dp_0'=4,'dp_1'=8,'tensor_0'=4,'tensor_1'=2] {'dp_0','dp_1'}, dimensions={0} | all-to-all | bytes 1310720 | tf_op jit(solution)/shard_map/all_to_all | solution.py:50
  118.8 28.5 %all_to_all.59 = f32[32,20,256]{2,1,0:T(8,128)S(1)} all-to-all(f32[32,20,256]{2,1,0:T(8,128)S(1)} %broadcast_in_dim.31), channel_id=1, replica_groups=mesh['dp_0'=4,'dp_1'=8,'tensor_0'=4,'tensor_1'=2] {'dp_0','dp_1'}, dimensions={0} | all-to-all | bytes 1310720 | tf_op jit(solution)/shard_map/all_to_all | solution.py:17
  147.5 1.2 convolution_bitcast_fusion
  148.8 1.5 broadcast_in_dim.32
  150.3 8.0 %all-to-all-start.6 = ((f32[8,256,256]{2,1,0:T(8,128)}), f32[8,256,256]{2,1,0:T(8,128)S(1)}, u32[]{:S(2)}, u32[]{:S(2)}) async-start(f32[8,256,256]{2,1,0:T(8,128)} %broadcast_in_dim.32), calls=%async_computation.6 | async-start | bytes 4194304 | tf_op jit(solution)/shard_map/all_to_all | solution.py:17
  158.3 1.5 copy.32
  159.7 0.9 div.28
  160.7 24.0 %all-to-all-done.6 = f32[8,256,256]{2,1,0:T(8,128)S(1)} async-done(((f32[8,256,256]{2,1,0:T(8,128)}), f32[8,256,256]{2,1,0:T(8,128)S(1)}, u32[]{:S(2)}, u32[]{:S(2)}) %all-to-all-start.6) | async-done | bytes 2097184 | tf_op jit(solution)/shard_map/all_to_all | solution.py:17
  185.0 11.7 %cholesky.50 = f32[128,128]{1,0:T(8,128)S(1)} custom-call(f32[128,128]{1,0:T(8,128)S(1)} %cholesky.118), custom_call_target="Cholesky" | custom-call | tf_op jit(solution)/shard_map/jit(cholesky)/cholesky | solution.py:85
  196.7 9.8 %custom-call.14 = f32[1,128,128]{1,2,0:T(8,128)S(1)} custom-call(f32[1,128,128]{2,1,0:T(8,128)S(1)} %get-tuple-element.41), custom_call_target="InvertDiagBlocksLowerTriangular" | custom-call | tf_op jit(solution)/shard_map/jit(cholesky)/cholesky | solution.py:85
  206.8 0.3 convolution_subtract_fusion.1
  207.0 11.7 %cholesky.105 = f32[128,128]{1,0:T(8,128)S(1)} custom-call(f32[128,128]{1,0:T(8,128)S(1)} %convolution_subtract_fusion.1), custom_call_target="Cholesky" | custom-call | tf_op jit(solution)/shard_map/jit(cholesky)/cholesky | solution.py:85
  218.8 0.7 compare_reduce_fusion
  220.8 3.8 %while.1 = (s32[]{:T(128)}, f32[256,256]{1,0:T(8,128)S(1)}, s32[2,2]{1,0:T(2,128)S(1)}, f32[2,128,128]{2,1,0:T(8,128)S(1)}, s32[]{:T(128)}) while((s32[]{:T(128)}, f32[256,256]{1,0:T(8,128)S(1)}, s32[2,2]{1,0:T(2,128)S(1)}, f32[2,128,128]{2,1,0:T(8,128)S(1)}, s32[]{:T(128)}) %tuple.33), condition=%wide.while_cond, body=%wide.while_body.sunk | while | flops 2 | bytes 131189 | solution.py:86
  220.8 0.6 fusion.24
  221.4 1.3 bitcast_dynamic-update-slice_fusion.2
  222.7 0.6 fusion.24
  223.3 1.3 bitcast_dynamic-update-slice_fusion.2
  224.6 19.9 %custom-call.15 = f32[2,128,128]{1,2,0:T(8,128)S(1)} custom-call(f32[2,128,128]{2,1,0:T(8,128)S(1)} %get-tuple-element.10), custom_call_target="InvertDiagBlocksLowerTriangular" | custom-call | tf_op jit(solution)/shard_map/triangular_solve | solution.py:86
  244.5 0.5 fusion
  245.0 0.7 convolution_subtract_fusion
  245.7 0.5 fusion.3
  246.2 10.5 %fusion.8 = f32[2048,256]{1,0:T(8,128)S(1)} fusion(f32[640,2048]{1,0:T(8,128)} %multiply_add_fusion, f32[640,128]{0,1:T(8,128)S(1)} %fusion.3, f32[640,128]{0,1:T(8,128)S(1)} %fusion), kind=kOutput, calls=%fused_computation.37 | convolution fusion | flops 4026695680 | bytes 7995392 | tf_op jit(solution)/shard_map/dot_general | solution.py:79
  256.8 29.8 %all_to_all.60 = f32[8,32,8,256]{3,2,1,0:T(8,128)S(1)} all-to-all(f32[8,32,8,256]{3,2,1,0:T(8,128)S(1)} %bitcast.59), channel_id=1, replica_groups=mesh['dp_0'=4,'dp_1'=8,'tensor_0'=4,'tensor_1'=2] {'tensor_0','tensor_1'}, dimensions={0} | all-to-all | bytes 4194304 | tf_op jit(solution)/shard_map/all_to_all | solution.py:50
  286.8 13.9 %all_to_all.61 = f32[32,8,256]{2,1,0:T(8,128)S(1)} all-to-all(f32[32,8,256]{2,1,0:T(8,128)S(1)} %reduce_sum.47), channel_id=1, replica_groups=mesh['dp_0'=4,'dp_1'=8,'tensor_0'=4,'tensor_1'=2] {'dp_0','dp_1'}, dimensions={0} | all-to-all | bytes 524288 | tf_op jit(solution)/shard_map/all_to_all | solution.py:68
  300.8 15.5 %all_to_all.62 = f32[32,8,256]{2,1,0:T(8,128)S(1)} all-to-all(f32[32,8,256]{2,1,0:T(8,128)S(1)} %broadcast_in_dim.33), channel_id=1, replica_groups=mesh['dp_0'=4,'dp_1'=8,'tensor_0'=4,'tensor_1'=2] {'dp_0','dp_1'}, dimensions={0} | all-to-all | bytes 524288 | tf_op jit(solution)/shard_map/all_to_all | solution.py:17
  316.3 1.5 broadcast_in_dim.34
  317.8 7.2 %all-to-all-start.10 = ((f32[8,32,8,256]{3,2,1,0:T(8,128)}), f32[8,32,8,256]{3,2,1,0:T(8,128)S(1)}, u32[]{:S(2)}, u32[]{:S(2)}) async-start(f32[8,32,8,256]{3,2,1,0:T(8,128)} %broadcast_in_dim.34), calls=%async_computation.10 | async-start | bytes 4194304 | tf_op jit(solution)/shard_map/all_to_all | solution.py:17
  325.1 1.1 copy.36
  326.1 25.2 %all-to-all-done.10 = f32[8,32,8,256]{3,2,1,0:T(8,128)S(1)} async-done(((f32[8,32,8,256]{3,2,1,0:T(8,128)}), f32[8,32,8,256]{3,2,1,0:T(8,128)S(1)}, u32[]{:S(2)}, u32[]{:S(2)}) %all-to-all-start.10) | async-done | bytes 2097184 | tf_op jit(solution)/shard_map/all_to_all | solution.py:17
  351.4 0.3 multiply_reduce_fusion
  351.7 0.6 copy-done.4
  352.4 11.9 %multiply_subtract_fusion = f32[640,2048]{1,0:T(8,128)} fusion(f32[640,2048]{1,0:T(8,128)} %multiply_add_fusion, f32[2048,256]{1,0:T(8,128)S(1)} %bitcast.56, f32[640,128]{0,1:T(8,128)S(1)} %copy-done.6, f32[640,128]{0,1:T(8,128)S(1)} %copy-done.4), kind=kOutput, calls=%fused_computation.2 | convolution fusion | flops 4029317120 | bytes 13238272 | tf_op jit(solution)/shard_map/dot_general | solution.py:112
  364.4 0.7 dynamic-slice_multiply_fusion
  (47 shorter events, 1.8 us)
Async XLA Ops:
  0.6 68.7 %copy-start = (bf16[1024,640]{1,0:T(8,128)(2,1)S(1)}, bf16[1024,640]{1,0:T(8,128)(2,1)}, u32[]{:S(2)}) copy-start(bf16[1024,640]{1,0:T(8,128)(2,1)} %param.4) | copy-start | bytes 3932164
  20.7 8.0 %copy-start.9 = (bf16[128,2048]{1,0:T(8,128)(2,1)S(1)}, bf16[128,2048]{1,0:T(8,128)(2,1)}, u32[]{:S(2)}) copy-start(bf16[128,2048]{1,0:T(8,128)(2,1)} %param.5) | copy-start | bytes 1572868
  30.3 29.7 %all-to-all-start = ((bf16[4,128,2048]{2,1,0:T(8,128)(2,1)}), bf16[4,128,2048]{2,1,0:T(8,128)(2,1)S(1)}, u32[]{:S(2)}, u32[]{:S(2)}) async-start(bf16[4,128,2048]{2,1,0:T(8,128)(2,1)} %broadcast_in_dim.27), calls=%async_computation | async-start | bytes 4194304 | tf_op jit(solution)/shard_map/all_to_all | solution.py:17
  60.5 8.8 %slice-start = ((s8[5242880]{0:T(1024)(128)(4,1)}), s8[4194304]{0:T(1024)(128)(4,1)S(1)}, s32[]{:S(2)}) async-start(s8[5242880]{0:T(1024)(128)(4,1)} %bitcast.62), calls=%async_computation.11 | async-start | bytes 8388608
  68.7 1.2 slice-start.1
  74.7 6.9 %copy-start.2 = (f32[4,2,256,256]{3,2,1,0:T(8,128)S(1)}, f32[4,2,256,256]{3,2,1,0:T(8,128)}, u32[]{:S(2)}) copy-start(f32[4,2,256,256]{3,2,1,0:T(8,128)} %copy.30) | copy-start | bytes 6291460
  147.5 2.8 copy-start.8
  150.3 34.3 %all-to-all-start.6 = ((f32[8,256,256]{2,1,0:T(8,128)}), f32[8,256,256]{2,1,0:T(8,128)S(1)}, u32[]{:S(2)}, u32[]{:S(2)}) async-start(f32[8,256,256]{2,1,0:T(8,128)} %broadcast_in_dim.32), calls=%async_computation.6 | async-start | bytes 4194304 | tf_op jit(solution)/shard_map/all_to_all | solution.py:17
  184.8 59.7 %copy-start.7 = (f32[640,256]{1,0:T(8,128)S(1)}, f32[640,256]{1,0:T(8,128)}, u32[]{:S(2)}) copy-start(f32[640,256]{1,0:T(8,128)} %div.28) | copy-start | bytes 1966084
  245.0 80.0 %copy-start.3 = (f32[640,128]{0,1:T(8,128)}, f32[640,128]{0,1:T(8,128)S(1)}, u32[]{:S(2)}) copy-start(f32[640,128]{0,1:T(8,128)S(1)} %fusion) | copy-start | bytes 983044
  246.2 78.8 %copy-start.5 = (f32[640,128]{0,1:T(8,128)}, f32[640,128]{0,1:T(8,128)S(1)}, u32[]{:S(2)}) copy-start(f32[640,128]{0,1:T(8,128)S(1)} %fusion.3) | copy-start | bytes 983044
  317.8 33.5 %all-to-all-start.10 = ((f32[8,32,8,256]{3,2,1,0:T(8,128)}), f32[8,32,8,256]{3,2,1,0:T(8,128)S(1)}, u32[]{:S(2)}, u32[]{:S(2)}) async-start(f32[8,32,8,256]{3,2,1,0:T(8,128)} %broadcast_in_dim.34), calls=%async_computation.10 | async-start | bytes 4194304 | tf_op jit(solution)/shard_map/all_to_all | solution.py:17
  351.4 1.0 copy-start.4
  351.4 1.1 copy-start.6
  352.4 12.7 %copy-start.1 = (bf16[1024,640]{1,0:T(8,128)(2,1)S(1)}, bf16[1024,640]{1,0:T(8,128)(2,1)}, u32[]{:S(2)}) copy-start(bf16[1024,640]{1,0:T(8,128)(2,1)} %param.4) | copy-start | bytes 3932164
where the time goes:
time: 366 us; the launch traced here: 365 us
  blocking collectives  153 us (42%)
  waiting for transfers between devices  72.2 us (20%)
  other arithmetic  55.7 us (15%)
  matrix products  37.7 us (10%)
  local copies, waits for them, and re-layouts  26 us (7%)
  starting transfers between devices  18.8 us (5%)
    all_to_all x5, blocking collectives, from_everyone(): return lax.all_to_all(copies, axis, split_axis=0, concat_axis=0, tiled=True)  79 us
    all_to_all x3, waiting for transfers between devices, from_everyone(): return lax.all_to_all(copies, axis, split_axis=0, concat_axis=0, tiled=True)  72.2 us
    all_to_all x2, blocking collectives, summed_on_arrival(): lax.all_to_all(blocks, axis, split_axis=0, concat_axis=0, tiled=True)  59.6 us
    another operation x6, other arithmetic, orthonormal(): chol = jnp.linalg.cholesky(gram)  34 us
    another operation x4, other arithmetic, orthonormal(): lax.linalg.triangular_solve(chol, left, left_side=False, lower=True, tran...  20 us
    all_to_all x3, starting transfers between devices, from_everyone(): return lax.all_to_all(copies, axis, split_axis=0, concat_axis=0, tiled=True)  18.8 us
    all_to_all x1, blocking collectives, summed_rows(): return jnp.sum(lax.all_to_all(own, far, 0, 0, tiled=True), axis=0)  13.9 us
    dot_general x1, matrix products, body(): jnp.dot(ortho, right.T, precision=HIGH, preferred_element_type=jnp.float32)  11.9 us
  transfers between devices with their start and end apart: 3, of which 3 were waited for; matrix products, arithmetic and copies ran while one was open for 2% of the time, Pallas kernels for 0%

commit v1 on v0

--- a/solution.py
+++ b/solution.py
@@ -1,15 +1,285 @@
 import jax
 import jax.numpy as jnp
 from jax import lax
+from jax.experimental import pallas as pl
+from jax.experimental.pallas import tpu as pltpu
 from jax.sharding import Mesh
 from jax.sharding import PartitionSpec as P
 
 DP = ("dp_0", "dp_1")
 TENSOR = ("tensor_0", "tensor_1")
 DP_TENSOR = ("dp_0", "dp_1", "tensor_0", "tensor_1")
-
-
 HIGH = lax.Precision.HIGHEST
+F32, BF16 = jnp.float32, jnp.bfloat16
+MESH = pl.DeviceIdType.MESH
+
+
+def halves(value):
+    high = value.astype(BF16)
+    return high, (value - high.astype(F32)).astype(BF16)
+
+
+def mxu(a, b):
+    return lax.dot_general(a, b, (((1,), (0,)), ((), ())), preferred_element_type=F32)
+
+
+class Place:
+    def __init__(self):
+        self.y, self.z = lax.axis_index("dp_0"), lax.axis_index("dp_1")
+        self.x, self.c = lax.axis_index("tensor_0"), lax.axis_index("tensor_1")
+        step = 1 - 2 * self.c
+        self.sib = 1 - self.c
+        self.xp, self.xm = lax.rem(self.x + step + 4, 4), lax.rem(self.x - step + 4, 4)
+        self.yp, self.ym = lax.rem(self.y + step + 4, 4), lax.rem(self.y - step + 4, 4)
+        self.xo, self.yo = lax.rem(self.x + 2, 4), lax.rem(self.y + 2, 4)
+
+    def zk(self, k):
+        return lax.rem(self.z + k, 8)
+
+
+def greet(me):
+    barrier = pltpu.get_barrier_semaphore()
+    targets = [{"tensor_1": me.sib}, {"tensor_0": me.xp}, {"tensor_0": me.xm}]
+    targets += [{"dp_0": me.yp}, {"dp_0": me.ym}]
+    targets += [{"dp_1": me.zk(k)} for k in range(1, 8)]
+    for target in targets:
+        pl.semaphore_signal(barrier, inc=1, device_id=target, device_id_type=MESH)
+    pl.semaphore_wait(barrier, len(targets))
+
+
+class Links:
+    def __init__(self, send, recv):
+        self.send, self.recv, self.used, self.sent = send, recv, 0, []
+
+    def to(self, src, dst, target):
+        copy = pltpu.make_async_remote_copy(
+            src_ref=src,
+            dst_ref=dst,
+            send_sem=self.send.at[self.used],
+            recv_sem=self.recv.at[self.used],
+            device_id=target,
+            device_id_type=MESH,
+        )
+        self.used += 1
+        copy.start()
+        self.sent.append(copy)
+        return copy
+
+    def finish(self):
+        for copy in self.sent:
+            copy.wait_send()
+
+
+class Gather:
+    def __init__(self, me, links, own, slot):
+        self.me, self.links, self.slot = me, links, slot
+        here = slot(me.x, me.c)
+        self.a = links.to(own, here, {"tensor_0": me.xp})
+        self.b = links.to(own, here, {"tensor_0": me.xm})
+        self.s0 = links.to(own, here, {"tensor_1": me.sib})
+
+    def first(self):
+        me = self.me
+        self.a.wait_recv()
+        block = self.slot(me.xm, me.c)
+        self.f = self.links.to(block, block, {"tensor_0": me.xp})
+        self.s1 = self.links.to(block, block, {"tensor_1": me.sib})
+
+    def second(self):
+        me = self.me
+        self.b.wait_recv()
+        block = self.slot(me.xp, me.c)
+        self.s2 = self.links.to(block, block, {"tensor_1": me.sib})
+
+    def third(self):
+        me = self.me
+        self.f.wait_recv()
+        block = self.slot(me.xo, me.c)
+        self.s3 = self.links.to(block, block, {"tensor_1": me.sib})
+
+    def rest(self):
+        for copy in (self.s0, self.s1, self.s2, self.s3):
+            copy.wait_recv()
+
+
+def left_kernel(
+    acts, og, mom, q, buf_out, left_out,
+    actsv, acts_t, buf, qg, qh, ql, yg, yh, yl, ogg,
+    part, r0, r1, r2, s1, chunk, zr, zs, full, send, recv, local,
+):
+    me = Place()
+    links = Links(send, recv)
+    own_q = qg.at[me.x * 2 + me.c]
+    own_rows = pl.ds(pl.multiple_of(me.c * 128, 128), 128)
+    own_og = ogg.at[me.x, own_rows]
+    loads = [
+        pltpu.make_async_copy(q, own_q, local.at[0]),
+        pltpu.make_async_copy(og, own_og, local.at[1]),
+        pltpu.make_async_copy(acts, actsv, local.at[2]),
+        pltpu.make_async_copy(mom, buf, local.at[3]),
+    ]
+    for load in loads:
+        load.start()
+    greet(me)
+    gq = Gather(me, links, q, lambda x, c: qg.at[x * 2 + c])
+    loads[2].wait()
+    for j in range(4):
+        acts_t[j] = actsv[256 * j : 256 * (j + 1), :].T
+    gq.first()
+    gq.second()
+    gq.third()
+    loads[0].wait()
+    gq.rest()
+
+    @pl.loop(0, 8)
+    def _(b):
+        high, low = halves(qg[b])
+        rows = pl.ds(pl.multiple_of(b * 256, 256), 256)
+        qh[rows], ql[rows] = high, low
+
+    loads[1].wait()
+    own = ogg[me.x, own_rows, :]
+    own_y = yg.at[me.x, own_rows]
+    yg[me.x, own_rows, :] = mxu(own, qh[...]) + mxu(own, ql[...])
+    gy = Gather(me, links, own_y, lambda x, c: yg.at[x, pl.ds(pl.multiple_of(c * 128, 128), 128)])
+    loads[3].wait()
+
+    def momentum_part(t):
+        rows = pl.ds(pl.multiple_of(t * 128, 128), 128)
+        high, low = halves(buf[rows, :])
+        acc = mxu(high, qh[...]) + mxu(high, ql[...]) + mxu(low, qh[...])
+        acc = acc * (0.95 / 32)
+        part[0, rows, :] = acc[:, :128]
+        part[1, rows, :] = acc[:, 128:]
+
+    pl.loop(0, 2)(momentum_part)
+    gy.first()
+    gy.second()
+    pl.loop(2, 5)(momentum_part)
+    gy.third()
+    gy.rest()
+    go = Gather(
+        me, links, og, lambda x, c: ogg.at[x, pl.ds(pl.multiple_of(c * 128, 128), 128)]
+    )
+    for j in range(4):
+        high, low = halves(yg[j])
+        yh[j], yl[j] = high, low
+
+    @pl.loop(0, 5)
+    def _(t):
+        rows = pl.ds(pl.multiple_of(t * 128, 128), 128)
+        acc = jnp.zeros((128, 256), F32)
+        for j in range(4):
+            lhs = acts_t[j, rows, :]
+            acc += mxu(lhs, yh[j]) + mxu(lhs, yl[j])
+        acc = acc * (1 / 32)
+        part[0, rows, :] += acc[:, :128]
+        part[1, rows, :] += acc[:, 128:]
+
+    def of_y(ref, y):
+        return ref.at[:, pl.ds(pl.multiple_of(y * 160, 32), 160)]
+
+    far = links.to(of_y(part, me.yo), r1, {"dp_0": me.yp})
+    near = links.to(of_y(part, me.ym), r0, {"dp_0": me.ym})
+    far.wait_recv()
+    s1[...] = r1[...] + of_y(part, me.yp)[...]
+    last = links.to(s1, r2, {"dp_0": me.yp})
+    near.wait_recv()
+    chunk[...] = r0[...] + of_y(part, me.y)[...]
+    last.wait_recv()
+    chunk[...] += r2[...]
+
+    def z_rows(z):
+        return z // 4, pl.multiple_of(lax.rem(z, 4) * 40, 8)
+
+    came = []
+    for k in range(1, 8):
+        half, row = z_rows(me.zk(k))
+        came.append(
+            links.to(chunk.at[half, pl.ds(row, 40)], zr.at[k - 1], {"dp_1": me.zk(k)})
+        )
+    go.first()
+    go.second()
+    half, row = z_rows(me.z)
+    for copy in came:
+        copy.wait_recv()
+    total = chunk[half, pl.ds(row, 40), :]
+    for k in range(7):
+        total += zr[k]
+    zs[...] = total
+    spot = full.at[half, pl.ds(pl.multiple_of(me.y * 160 + row, 8), 40)]
+    came = [links.to(zs, spot, {"dp_1": me.zk(k)}) for k in range(1, 8)]
+    spot[...] = total
+    for copy in came:
+        copy.wait_recv()
+    mine = of_y(full, me.y)
+    up = links.to(mine, mine, {"dp_0": me.yp})
+    down = links.to(mine, mine, {"dp_0": me.ym})
+    go.third()
+    up.wait_recv()
+    block = of_y(full, me.ym)
+    far = links.to(block, block, {"dp_0": me.yp})
+    go.rest()
+
+    @pl.loop(0, 8)
+    def _(n):
+        cols = pl.ds(pl.multiple_of(n * 256, 256), 256)
+        acc = 0.95 * buf[:, cols]
+        for j in range(4):
+            acc += mxu(acts_t[j], ogg[j, :, cols])
+        buf[:, cols] = acc
+
+    store = pltpu.make_async_copy(buf, buf_out, local.at[4])
+    store.start()
+    down.wait_recv()
+    far.wait_recv()
+    left_out[:, :128] = full[0]
+    left_out[:, 128:] = full[1]
+    store.wait()
+    links.finish()
+
+
+def buffer_and_left(acts, out_grad, momentum, q_basis):
+    any_space = pl.BlockSpec(memory_space=pl.ANY)
+    copies = 21 + 3 + 14 + 3
+    scratch = [
+        pltpu.VMEM((1024, 640), BF16),
+        pltpu.VMEM((4, 640, 256), BF16),
+        pltpu.VMEM((640, 2048), F32),
+        pltpu.VMEM((8, 256, 256), F32),
+        pltpu.VMEM((2048, 256), BF16),
+        pltpu.VMEM((2048, 256), BF16),
+        pltpu.VMEM((4, 256, 256), F32),
+        pltpu.VMEM((4, 256, 256), BF16),
+        pltpu.VMEM((4, 256, 256), BF16),
+        pltpu.VMEM((4, 256, 2048), BF16),
+        pltpu.VMEM((2, 640, 128), F32),
+        pltpu.VMEM((2, 160, 128), F32),
+        pltpu.VMEM((2, 160, 128), F32),
+        pltpu.VMEM((2, 160, 128), F32),
+        pltpu.VMEM((2, 160, 128), F32),
+        pltpu.VMEM((2, 160, 128), F32),
+        pltpu.VMEM((7, 40, 128), F32),
+        pltpu.VMEM((40, 128), F32),
+        pltpu.VMEM((2, 640, 128), F32),
+        pltpu.SemaphoreType.DMA((copies,)),
+        pltpu.SemaphoreType.DMA((copies,)),
+        pltpu.SemaphoreType.DMA((5,)),
+    ]
+    return pl.pallas_call(
+        left_kernel,
+        out_shape=(
+            jax.ShapeDtypeStruct((640, 2048), F32),
+            jax.ShapeDtypeStruct((640, 256), F32),
+        ),
+        in_specs=[any_space] * 4,
+        out_specs=(any_space, pl.BlockSpec(memory_space=pltpu.VMEM)),
+        scratch_shapes=scratch,
+        compiler_params=pltpu.CompilerParams(
+            collective_id=0, has_side_effects=True, vmem_limit_bytes=48 * 2**20
+        ),
+        name="buffer_and_left",
+    )(acts, out_grad, momentum, q_basis)
 
 
 def from_everyone(value, axis):
@@ -89,20 +359,7 @@
 def body(acts, out_grad, momentum, q_basis):
     width_out = out_grad.shape[1]
     replicas = lax.axis_size(DP)
-    grad = lax.dot_general(
-        acts,
-        whole_of(out_grad, ("tensor_0", "tensor_1"), 0),
-        (((0,), (0,)), ((), ())),
-        preferred_element_type=jnp.float32,
-    )
-    buffer = 0.95 * momentum + grad
-    left_local = jnp.dot(
-        buffer,
-        whole_of(q_basis, ("tensor_0", "tensor_1"), 0),
-        precision=HIGH,
-        preferred_element_type=jnp.float32,
-    )
-    left = sum_by_parts(left_local, DP) / replicas
+    buffer, left = buffer_and_left(acts, out_grad, momentum, q_basis)
     gram = of_everyone(contract_rows(left, left), TENSOR)
     ortho = orthonormal(left, gram)
     right = (

time: 366 us -> 288 us (0.79)
  blocking collectives: 153 us -> 59.4 us
  Pallas kernels: 0 us -> 66.3 us
  waiting for transfers between devices: 72.2 us -> 49.6 us
  local copies, waits for them, and re-layouts: 26 us -> 12.8 us
  matrix products: 37.7 us -> 25.5 us
  starting transfers between devices: 18.8 us -> 14.9 us
    pallas_call x0 -> x1, Pallas kernels: none -> 66.3 us  [buffer_and_left(): pl.pallas_call(left_kernel, out_shape=(jax.ShapeDtypeStruct((640, 2048),...]
    all_to_all x5 -> x1, blocking collectives: 79 us -> 15.5 us  [from_everyone(): return lax.all_to_all(copies, axis, split_axis=0, concat_axis=0, tiled=True)]
    all_to_all x2 -> x1, blocking collectives: 59.6 us -> 29.8 us  [summed_on_arrival(): lax.all_to_all(blocks, axis, split_axis=0, concat_axis=0, tiled=True)]
    all_to_all x3 -> x2, waiting for transfers between devices: 72.2 us -> 49.6 us  [from_everyone(): return lax.all_to_all(copies, axis, split_axis=0, concat_axis=0, tiled=True)]
    dot_general x2 -> x0, matrix products: 12 us -> none  [the longest x1 7.24 us: body(): jnp.dot(buffer, whole_of(q_basis, ('tensor_0', 'tensor_1'), 0), precision...]
    dot_general x1 -> x0, local copies, waits for them, and re-layouts: 6.86 us -> none  [body(): jnp.dot(buffer, whole_of(q_basis, ('tensor_0', 'tensor_1'), 0), precision...]
    all_to_all x3 -> x2, starting transfers between devices: 18.8 us -> 14.9 us  [from_everyone(): return lax.all_to_all(copies, axis, split_axis=0, concat_axis=0, tiled=True)]
  transfers between devices with their start and end apart: 3 -> 2, of which waited for: 3 -> 2; matrix products, arithmetic and copies ran while one was open for 2% -> 1% of each run, Pallas kernels for 0% -> 0%
where the time goes in v1:
time: 288 us; the launch traced here: 287 us
  Pallas kernels  66.3 us (23%)
  blocking collectives  59.4 us (21%)
  other arithmetic  56.2 us (20%)
  waiting for transfers between devices  49.6 us (17%)
  matrix products  25.5 us (9%)
  starting transfers between devices  14.9 us (5%)
  local copies, waits for them, and re-layouts  12.8 us (4%)
    pallas_call x1, Pallas kernels, buffer_and_left(): pl.pallas_call(left_kernel, out_shape=(jax.ShapeDtypeStruct((640, 2048),...  66.3 us
    all_to_all x2, waiting for transfers between devices, from_everyone(): return lax.all_to_all(copies, axis, split_axis=0, concat_axis=0, tiled=True)  49.6 us
    another operation x6, other arithmetic, orthonormal(): chol = jnp.linalg.cholesky(gram)  33.9 us
    all_to_all x1, blocking collectives, summed_on_arrival(): lax.all_to_all(blocks, axis, split_axis=0, concat_axis=0, tiled=True)  29.8 us
    another operation x4, other arithmetic, orthonormal(): lax.linalg.triangular_solve(chol, left, left_side=False, lower=True, tran...  20.8 us
    all_to_all x1, blocking collectives, from_everyone(): return lax.all_to_all(copies, axis, split_axis=0, concat_axis=0, tiled=True)  15.5 us
    all_to_all x2, starting transfers between devices, from_everyone(): return lax.all_to_all(copies, axis, split_axis=0, concat_axis=0, tiled=True)  14.9 us
    all_to_all x1, blocking collectives, summed_rows(): return jnp.sum(lax.all_to_all(own, far, 0, 0, tiled=True), axis=0)  14.1 us
  transfers between devices with their start and end apart: 2, of which 2 were waited for; matrix products, arithmetic and copies ran while one was open for 1% of the time, Pallas kernels for 0%

profile of v1, /device:TPU:1, one launch (start us, length us, event | category | flops | bytes accessed | tf_op | source)
XLA Modules:
  0.0 287.0 jit_solution(4988889707142545148)
XLA Ops:
  0.6 0.0 copy-start
  0.6 1.3 copy-done
  1.9 0.0 copy-start.1
  2.0 1.0 copy-done.1
  3.0 0.0 copy-start.2
  3.0 0.9 copy-done.2
  3.9 66.3 %buffer_and_left.1 = (f32[640,2048]{1,0:T(8,128)}, f32[640,256]{1,0:T(8,128)S(1)}) custom-call(bf16[1024,640]{1,0:T(8,128)(2,1)S(1)} %copy-done, bf16[128,2048]{1,0:T(8,128)(2,1)S(1)} %copy-done.1, f32[640,2048]{1,0:T(8,128)} %mom.1, f32[256,256]{1,0:T(8,128)S(1)} %copy-done.2), custom_call_target="tpu_custom_call" | custom-call | tf_op jit(solution)/shard_map/buffer_and_left/pallas_call | solution.py:269
  70.3 1.2 fusion.10
  71.5 1.5 broadcast_in_dim.12
  73.0 7.8 %all-to-all-start = ((f32[8,256,256]{2,1,0:T(8,128)}), f32[8,256,256]{2,1,0:T(8,128)S(1)}, u32[]{:S(2)}, u32[]{:S(2)}) async-start(f32[8,256,256]{2,1,0:T(8,128)} %broadcast_in_dim.12), calls=%async_computation | async-start | bytes 4194304 | tf_op jit(solution)/shard_map/all_to_all | solution.py:287
  80.8 26.3 %all-to-all-done = f32[8,256,256]{2,1,0:T(8,128)S(1)} async-done(((f32[8,256,256]{2,1,0:T(8,128)}), f32[8,256,256]{2,1,0:T(8,128)S(1)}, u32[]{:S(2)}, u32[]{:S(2)}) %all-to-all-start) | async-done | bytes 2097184 | tf_op jit(solution)/shard_map/all_to_all | solution.py:287
  107.1 0.1 reduce_sum.36
  107.3 0.1 copy.16
  107.5 11.7 %cholesky.50 = f32[128,128]{1,0:T(8,128)S(1)} custom-call(f32[128,128]{1,0:T(8,128)S(1)} %cholesky.118), custom_call_target="Cholesky" | custom-call | tf_op jit(solution)/shard_map/jit(cholesky)/cholesky | solution.py:355
  119.2 9.8 %custom-call.14 = f32[1,128,128]{1,2,0:T(8,128)S(1)} custom-call(f32[1,128,128]{2,1,0:T(8,128)S(1)} %get-tuple-element.42), custom_call_target="InvertDiagBlocksLowerTriangular" | custom-call | tf_op jit(solution)/shard_map/jit(cholesky)/cholesky | solution.py:355
  129.0 0.2 constant_dynamic-update-slice_fusion
  129.3 0.3 convolution_subtract_fusion.1
  129.5 11.7 %cholesky.105 = f32[128,128]{1,0:T(8,128)S(1)} custom-call(f32[128,128]{1,0:T(8,128)S(1)} %convolution_subtract_fusion.1), custom_call_target="Cholesky" | custom-call | tf_op jit(solution)/shard_map/jit(cholesky)/cholesky | solution.py:355
  141.3 0.6 compare_reduce_fusion
  143.3 0.1 triangular_solve.58
  143.3 4.0 %while.1 = (s32[]{:T(128)}, f32[256,256]{1,0:T(8,128)S(1)}, s32[2,2]{1,0:T(2,128)S(1)}, f32[2,128,128]{2,1,0:T(8,128)S(1)}, s32[]{:T(128)}) while((s32[]{:T(128)}, f32[256,256]{1,0:T(8,128)S(1)}, s32[2,2]{1,0:T(2,128)S(1)}, f32[2,128,128]{2,1,0:T(8,128)S(1)}, s32[]{:T(128)}) %tuple.32), condition=%wide.while_cond, body=%wide.while_body.sunk | while | flops 2 | bytes 131189 | solution.py:356
  143.3 0.6 fusion.20
  143.9 1.4 bitcast_dynamic-update-slice_fusion.2
  145.3 0.6 fusion.20
  145.9 1.4 bitcast_dynamic-update-slice_fusion.2
  147.3 19.9 %custom-call.15 = f32[2,128,128]{1,2,0:T(8,128)S(1)} custom-call(f32[2,128,128]{2,1,0:T(8,128)S(1)} %get-tuple-element.14), custom_call_target="InvertDiagBlocksLowerTriangular" | custom-call | tf_op jit(solution)/shard_map/triangular_solve | solution.py:356
  167.2 0.5 fusion
  167.7 0.7 convolution_subtract_fusion
  168.4 0.5 fusion.3
  168.9 10.3 %fusion.8 = f32[2048,256]{1,0:T(8,128)S(1)} fusion(f32[640,2048]{1,0:T(8,128)} %get-tuple-element.5, f32[640,128]{0,1:T(8,128)S(1)} %fusion.3, f32[640,128]{0,1:T(8,128)S(1)} %fusion), kind=kOutput, calls=%fused_computation.34 | convolution fusion | flops 4026695680 | bytes 7995392 | tf_op jit(solution)/shard_map/dot_general | solution.py:349
  179.3 0.2 copy.24
  179.5 29.8 %all_to_all.25 = f32[8,32,8,256]{3,2,1,0:T(8,128)S(1)} all-to-all(f32[8,32,8,256]{3,2,1,0:T(8,128)S(1)} %bitcast.44), channel_id=1, replica_groups=mesh['dp_0'=4,'dp_1'=8,'tensor_0'=4,'tensor_1'=2] {'tensor_0','tensor_1'}, dimensions={0} | all-to-all | bytes 4194304 | tf_op jit(solution)/shard_map/all_to_all | solution.py:320
  209.2 0.1 reduce_sum.37
  209.4 14.1 %all_to_all.26 = f32[32,8,256]{2,1,0:T(8,128)S(1)} all-to-all(f32[32,8,256]{2,1,0:T(8,128)S(1)} %reduce_sum.37), channel_id=1, replica_groups=mesh['dp_0'=4,'dp_1'=8,'tensor_0'=4,'tensor_1'=2] {'dp_0','dp_1'}, dimensions={0} | all-to-all | bytes 524288 | tf_op jit(solution)/shard_map/all_to_all | solution.py:338
  223.5 15.5 %all_to_all.27 = f32[32,8,256]{2,1,0:T(8,128)S(1)} all-to-all(f32[32,8,256]{2,1,0:T(8,128)S(1)} %broadcast_in_dim.13), channel_id=1, replica_groups=mesh['dp_0'=4,'dp_1'=8,'tensor_0'=4,'tensor_1'=2] {'dp_0','dp_1'}, dimensions={0} | all-to-all | bytes 524288 | tf_op jit(solution)/shard_map/all_to_all | solution.py:287
  239.1 1.5 broadcast_in_dim.14
  240.6 7.2 %all-to-all-start.4 = ((f32[8,32,8,256]{3,2,1,0:T(8,128)}), f32[8,32,8,256]{3,2,1,0:T(8,128)S(1)}, u32[]{:S(2)}, u32[]{:S(2)}) async-start(f32[8,32,8,256]{3,2,1,0:T(8,128)} %broadcast_in_dim.14), calls=%async_computation.4 | async-start | bytes 4194304 | tf_op jit(solution)/shard_map/all_to_all | solution.py:287
  247.7 0.9 pad_maximum_fusion
  248.6 2.2 copy.19
  250.8 23.3 %all-to-all-done.4 = f32[8,32,8,256]{3,2,1,0:T(8,128)S(1)} async-done(((f32[8,32,8,256]{3,2,1,0:T(8,128)}), f32[8,32,8,256]{3,2,1,0:T(8,128)S(1)}, u32[]{:S(2)}, u32[]{:S(2)}) %all-to-all-start.4) | async-done | bytes 2097184 | tf_op jit(solution)/shard_map/all_to_all | solution.py:287
  274.1 0.3 multiply_reduce_fusion
  274.4 11.8 %multiply_subtract_fusion = f32[640,2048]{1,0:T(8,128)} fusion(f32[640,2048]{1,0:T(8,128)} %get-tuple-element.5, f32[2048,256]{1,0:T(8,128)S(1)} %bitcast.42, f32[640,128]{0,1:T(8,128)S(1)} %fusion.3, f32[640,128]{0,1:T(8,128)S(1)} %fusion), kind=kOutput, calls=%fused_computation.2 | convolution fusion | flops 4029317120 | bytes 13238272 | tf_op jit(solution)/shard_map/dot_general | solution.py:369
  286.3 0.7 dynamic-slice_multiply_fusion
  (13 shorter events, 0.2 us)
Async XLA Ops:
  0.6 1.3 copy-start
  1.9 1.0 copy-start.1
  3.0 0.9 copy-start.2
  73.0 34.1 %all-to-all-start = ((f32[8,256,256]{2,1,0:T(8,128)}), f32[8,256,256]{2,1,0:T(8,128)S(1)}, u32[]{:S(2)}, u32[]{:S(2)}) async-start(f32[8,256,256]{2,1,0:T(8,128)} %broadcast_in_dim.12), calls=%async_computation | async-start | bytes 4194304 | tf_op jit(solution)/shard_map/all_to_all | solution.py:287
  240.6 33.5 %all-to-all-start.4 = ((f32[8,32,8,256]{3,2,1,0:T(8,128)}), f32[8,32,8,256]{3,2,1,0:T(8,128)S(1)}, u32[]{:S(2)}, u32[]{:S(2)}) async-start(f32[8,32,8,256]{3,2,1,0:T(8,128)} %broadcast_in_dim.14), calls=%async_computation.4 | async-start | bytes 4194304 | tf_op jit(solution)/shard_map/all_to_all | solution.py:287

commit v2 on v1

v2 whole, which is shorter than its diff:
```python
import jax
import jax.numpy as jnp
from jax import lax
from jax.experimental import pallas as pl
from jax.experimental.pallas import tpu as pltpu
from jax.sharding import Mesh
from jax.sharding import PartitionSpec as P

DP = ("dp_0", "dp_1")
TENSOR = ("tensor_0", "tensor_1")
DP_TENSOR = ("dp_0", "dp_1", "tensor_0", "tensor_1")
HIGH = lax.Precision.HIGHEST
F32, BF16 = jnp.float32, jnp.bfloat16
MESH = pl.DeviceIdType.MESH


def halves(value):
    high = value.astype(BF16)
    return high, (value - high.astype(F32)).astype(BF16)


def mxu(a, b):
    return lax.dot_general(a, b, (((1,), (0,)), ((), ())), preferred_element_type=F32)


class Place:
    def __init__(self):
        self.y, self.z = lax.axis_index("dp_0"), lax.axis_index("dp_1")
        self.x, self.c = lax.axis_index("tensor_0"), lax.axis_index("tensor_1")
        step = 1 - 2 * self.c
        self.sib = 1 - self.c
        self.xp, self.xm = lax.rem(self.x + step + 4, 4), lax.rem(self.x - step + 4, 4)
        self.yp, self.ym = lax.rem(self.y + step + 4, 4), lax.rem(self.y - step + 4, 4)
        self.xo, self.yo = lax.rem(self.x + 2, 4), lax.rem(self.y + 2, 4)

    def tensor_peers(self):
        peers = [{"tensor_1": self.sib}]
        for n in range(1, 4):
            there = lax.rem(self.x + n, 4)
            peers.append({"tensor_0": there, "tensor_1": self.c})
            peers.append({"tensor_0": there, "tensor_1": self.sib})
        return peers

    def zk(self, k):
        return lax.rem(self.z + k, 8)


def greet(me):
    barrier = pltpu.get_barrier_semaphore()
    targets = me.tensor_peers()
    targets += [{"dp_0": me.yp}, {"dp_0": me.ym}]
    targets += [{"dp_1": me.zk(k)} for k in range(1, 8)]
    for target in targets:
        pl.semaphore_signal(barrier, inc=1, device_id=target, device_id_type=MESH)
    pl.semaphore_wait(barrier, len(targets))


class Links:
    def __init__(self, send, recv):
        self.send, self.recv, self.used, self.sent = send, recv, 0, []

    def to(self, src, dst, target):
        copy = pltpu.make_async_remote_copy(
            src_ref=src,
            dst_ref=dst,
            send_sem=self.send.at[self.used],
            recv_sem=self.recv.at[self.used],
            device_id=target,
            device_id_type=MESH,
        )
        self.used += 1
        copy.start()
        self.sent.append(copy)
        return copy

    def finish(self):
        for copy in self.sent:
            copy.wait_send()


class Gather:
    def __init__(self, me, links, own, slot):
        self.me, self.links, self.slot = me, links, slot
        here = slot(me.x, me.c)
        self.a = links.to(own, here, {"tensor_0": me.xp})
        self.b = links.to(own, here, {"tensor_0": me.xm})
        self.s0 = links.to(own, here, {"tensor_1": me.sib})

    def first(self):
        me = self.me
        self.a.wait_recv()
        block = self.slot(me.xm, me.c)
        self.f = self.links.to(block, block, {"tensor_0": me.xp})
        self.s1 = self.links.to(block, block, {"tensor_1": me.sib})

    def second(self):
        me = self.me
        self.b.wait_recv()
        block = self.slot(me.xp, me.c)
        self.s2 = self.links.to(block, block, {"tensor_1": me.sib})

    def third(self):
        me = self.me
        self.f.wait_recv()
        block = self.slot(me.xo, me.c)
        self.s3 = self.links.to(block, block, {"tensor_1": me.sib})

    def rest(self):
        for copy in (self.s0, self.s1, self.s2, self.s3):
            copy.wait_recv()


class RingSum:
    def __init__(self, links, axis, places, src, came, stage):
        own, plus, minus, far = places
        self.links, self.axis, self.src = links, axis, src
        self.own, self.plus, self.came, self.stage = own, plus, came, stage
        self.far = links.to(src(far), came.at[0], {axis: plus})
        self.near = links.to(src(minus), came.at[1], {axis: minus})

    def middle(self):
        self.far.wait_recv()
        self.stage[...] = self.came[0] + self.src(self.plus)[...]
        self.last = self.links.to(self.stage, self.came.at[2], {self.axis: self.plus})

    def total(self):
        self.near.wait_recv()
        self.last.wait_recv()
        return self.src(self.own)[...] + self.came[1] + self.came[2]


class RingSpread:
    def __init__(self, links, axis, places, slot):
        own, plus, minus, _ = places
        self.links, self.axis, self.plus = links, axis, plus
        self.from_minus = slot(minus)
        self.up = links.to(slot(own), slot(own), {axis: plus})
        self.down = links.to(slot(own), slot(own), {axis: minus})

    def middle(self):
        self.up.wait_recv()
        self.far = self.links.to(self.from_minus, self.from_minus, {self.axis: self.plus})

    def finish(self):
        self.down.wait_recv()
        self.far.wait_recv()


def three(a, b, dims=((1,), (0,))):
    dot = lambda p, q: lax.dot_general(p, q, (dims, ((), ())), preferred_element_type=F32)
    return dot(a[0], b[0]) + dot(a[0], b[1]) + dot(a[1], b[0])


def rows_at(start, size, unit=8):
    return pl.ds(pl.multiple_of(start, unit), size)


def eliminate(d):
    lane = lax.broadcasted_iota(jnp.int32, (64, 128), 1)
    row = lax.broadcasted_iota(jnp.int32, (64, 128), 0)
    e = jnp.where(lane < 64, d, jnp.where(lane - 64 == row, 1.0, 0.0).astype(F32))

    def panel(p, e):
        live = 64 - 8 * p
        for first in range(0, 8, 8):
            cols = [jnp.broadcast_to(e[:, j : j + 1], (64, 128)) for j in range(first, first + 8)]
            for n, col in enumerate(cols):
                j = first + n
                weight = pl.reciprocal(col[j : j + 1])
                factor = jnp.where((row > j) & (row < live), col, 0.0) * weight
                e = e - factor * e[j : j + 1]
                for m in range(n + 1, 8):
                    cols[m] = cols[m] - factor * col[first + m : first + m + 1]
        e = pltpu.roll(e, 120, 1)
        return jnp.concatenate([e[8:], e[:8]], axis=0)

    e = lax.fori_loop(0, 8, panel, e)
    v = e[:, :64]
    diag = jnp.sum(jnp.where(lane - 64 == row, e, 0.0), axis=1, keepdims=True)
    return v * lax.rsqrt(diag)


def exact(a, b, dims=((1,), (0,))):
    return lax.dot_general(a, b, (dims, ((), ())), precision=HIGH, preferred_element_type=F32)


def factor_block(k, a, inv):
    rows = slice(64 * k, 64 * k + 64)
    block = a[rows, 128 * (k // 2) : 128 * (k // 2) + 128]
    if k % 2:
        block = pltpu.roll(block, 64, 1)
    v = eliminate(block)
    inv_row = exact(v, inv[rows, :])
    inv[rows, :] = inv_row
    if k < 3:
        u = exact(v, a[rows, :])
        below = u.T[64 * (k + 1) :, :]
        rest = slice(64 * (k + 1), 256)
        a[rest, :] = a[rest, :] - exact(below, u)
        inv[rest, :] = inv[rest, :] - exact(below, inv_row)


def step_kernel(
    acts, og, mom, q, new_out, ortho_out, q_out,
    actsv, acts_t, buf, qg, qh, ql, yg, yh, yl, ogg,
    part, r_left, s1, chunk, zr, zs, full,
    lh, ll, lth, ltl, gram, gram_r, gram_x, gram_f, a, inv,
    cc, c_sib, c_sum, rx, sx, tx, ry, sy, ty, rxy, sxy, ryx, syx,
    rest, zr2, zs2, all_z, own_right, wide, sq, ob,
    send, recv, local,
):
    me = Place()
    links = Links(send, recv)
    own_q = qg.at[me.x * 2 + me.c]
    own_rows = pl.ds(pl.multiple_of(me.c * 128, 128), 128)
    own_og = ogg.at[me.x, own_rows]
    loads = [
        pltpu.make_async_copy(q, own_q, local.at[0]),
        pltpu.make_async_copy(og, own_og, local.at[1]),
        pltpu.make_async_copy(acts, actsv, local.at[2]),
        pltpu.make_async_copy(mom, buf, local.at[3]),
    ]
    for load in loads:
        load.start()
    greet(me)
    gq = Gather(me, links, q, lambda x, c: qg.at[x * 2 + c])
    loads[2].wait()
    for j in range(4):
        acts_t[j] = actsv[256 * j : 256 * (j + 1), :].T
    gq.first()
    gq.second()
    gq.third()
    loads[0].wait()
    gq.rest()

    @pl.loop(0, 8)
    def _(b):
        high, low = halves(qg[b])
        rows = pl.ds(pl.multiple_of(b * 256, 256), 256)
        qh[rows], ql[rows] = high, low

    loads[1].wait()
    own = ogg[me.x, own_rows, :]
    own_y = yg.at[me.x, own_rows]
    yg[me.x, own_rows, :] = mxu(own, qh[...]) + mxu(own, ql[...])
    gy = Gather(me, links, own_y, lambda x, c: yg.at[x, pl.ds(pl.multiple_of(c * 128, 128), 128)])
    loads[3].wait()

    def momentum_part(t):
        rows = pl.ds(pl.multiple_of(t * 128, 128), 128)
        high, low = halves(buf[rows, :])
        acc = mxu(high, qh[...]) + mxu(high, ql[...]) + mxu(low, qh[...])
        acc = acc * (0.95 / 32)
        part[0, rows, :] = acc[:, :128]
        part[1, rows, :] = acc[:, 128:]

    pl.loop(0, 2)(momentum_part)
    gy.first()
    gy.second()
    pl.loop(2, 5)(momentum_part)
    gy.third()
    gy.rest()
    go = Gather(
        me, links, og, lambda x, c: ogg.at[x, pl.ds(pl.multiple_of(c * 128, 128), 128)]
    )
    for j in range(4):
        high, low = halves(yg[j])
        yh[j], yl[j] = high, low

    @pl.loop(0, 5)
    def _(t):
        rows = pl.ds(pl.multiple_of(t * 128, 128), 128)
        acc = jnp.zeros((128, 256), F32)
        for j in range(4):
            lhs = acts_t[j, rows, :]
            acc += mxu(lhs, yh[j]) + mxu(lhs, yl[j])
        acc = acc * (1 / 32)
        part[0, rows, :] += acc[:, :128]
        part[1, rows, :] += acc[:, 128:]

    def of_y(ref, y):
        return ref.at[:, pl.ds(pl.multiple_of(y * 160, 32), 160)]

    ys, xs = (me.y, me.yp, me.ym, me.yo), (me.x, me.xp, me.xm, me.xo)
    ring = RingSum(links, "dp_0", ys, lambda y: of_y(part, y), r_left, s1)
    ring.middle()
    chunk[...] = ring.total()

    def z_rows(z):
        return z // 4, pl.multiple_of(lax.rem(z, 4) * 40, 8)

    came = []
    for k in range(1, 8):
        half, row = z_rows(me.zk(k))
        came.append(
            links.to(chunk.at[half, pl.ds(row, 40)], zr.at[k - 1], {"dp_1": me.zk(k)})
        )
    go.first()
    go.second()
    half, row = z_rows(me.z)
    for copy in came:
        copy.wait_recv()
    total = chunk[half, pl.ds(row, 40), :]
    for k in range(7):
        total += zr[k]
    zs[...] = total
    spot = full.at[half, pl.ds(pl.multiple_of(me.y * 160 + row, 8), 40)]
    came = [links.to(zs, spot, {"dp_1": me.zk(k)}) for k in range(1, 8)]
    spot[...] = total
    for copy in came:
        copy.wait_recv()
    spread = RingSpread(links, "dp_0", ys, lambda y: of_y(full, y))
    go.third()
    spread.middle()
    go.rest()

    @pl.loop(0, 8)
    def _(n):
        cols = pl.ds(pl.multiple_of(n * 256, 256), 256)
        acc = 0.95 * buf[:, cols]
        for j in range(4):
            acc += mxu(acts_t[j], ogg[j, :, cols])
        buf[:, cols] = acc

    spread.finish()
    for half in range(2):
        cols = slice(128 * half, 128 * half + 128)
        lh[:, cols], ll[:, cols] = halves(full[half])
        lth[cols, :], ltl[cols, :] = halves(full[half].T)

    gram[...] = three((lth[...], ltl[...]), (lh[...], ll[...]))
    pair = links.to(gram, gram_r, {"tensor_1": me.sib})

    def product_with(core):
        @pl.loop(0, 4)
        def _(n):
            cols = rows_at((2 * n + core) * 256, 256, 256)
            block = three((lth[...], ltl[...]), halves(buf[:, cols]))
            cc[n, core] = block.T

    product_with(me.sib)
    swap = links.to(cc.at[:, me.sib], c_sib, {"tensor_1": me.sib})
    pair.wait_recv()
    half_rows = rows_at(me.c * 128, 128)
    gram_x[me.x] = gram[half_rows, :] + gram_r[half_rows, :]
    gram_spread = RingSpread(links, "tensor_0", xs, lambda x: gram_x.at[x])
    product_with(me.c)
    gram_spread.middle()
    swap.wait_recv()
    c_sum[...] = cc[:, me.c].reshape(4, 2, 128, 256) + c_sib[...].reshape(4, 2, 128, 256)
    x_first = RingSum(links, "tensor_0", xs, lambda x: c_sum.at[x, 0], rx, sx)
    y_first = RingSum(
        links, "dp_0", ys, lambda y: c_sum.at[:, 1, rows_at(y * 32, 32)], ry, sy
    )
    gram_spread.finish()
    gram_f[me.c] = ((gram_x[0] + gram_x[1]) + gram_x[2]) + gram_x[3]
    here = gram_f.at[me.c]
    whole = links.to(here, here, {"tensor_1": me.sib})
    same = lax.broadcasted_iota(jnp.int32, (256, 256), 0) == lax.broadcasted_iota(
        jnp.int32, (256, 256), 1
    )
    inv[...] = jnp.where(same, 1.0, 0.0).astype(F32)
    y_first.middle()
    x_first.middle()
    whole.wait_recv()
    a[:128, :] = gram_f[0]
    a[128:, :] = gram_f[1]

    factor_block(0, a, inv)
    tx[...] = x_first.total()
    then_y = RingSum(links, "dp_0", ys, lambda y: tx.at[rows_at(y * 32, 32)], ryx, syx)
    ty[...] = y_first.total()
    then_x = RingSum(links, "tensor_0", xs, lambda x: ty.at[x], rxy, sxy)
    factor_block(1, a, inv)
    then_y.middle()
    then_x.middle()
    factor_block(2, a, inv)
    rest[:32, :] = then_y.total()
    rest[32:, :] = then_x.total()
    came = [
        links.to(rest.at[rows_at(me.zk(k) * 8, 8)], zr2.at[k - 1], {"dp_1": me.zk(k)})
        for k in range(1, 8)
    ]
    factor_block(3, a, inv)
    for copy in came:
        copy.wait_recv()
    total = rest[rows_at(me.z * 8, 8), :]
    for k in range(7):
        total += zr2[k]
    total = total * (1 / 32)
    zs2[...] = total
    spot = all_z.at[rows_at(me.z * 8, 8)]
    came = [links.to(zs2, spot, {"dp_1": me.zk(k)}) for k in range(1, 8)]
    spot[...] = total
    inverse = halves(inv[...])
    across = ((1,), (1,))
    for copy in came:
        copy.wait_recv()
    mine = three(halves(all_z[...]), inverse, across)
    own_right[0, rows_at(me.y * 32, 32), :] = mine[:32]
    own_right[1, rows_at(me.y * 32, 32), :] = mine[32:]
    right_y = RingSpread(
        links, "dp_0", ys, lambda y: own_right.at[:, rows_at(y * 32, 32)]
    )
    ortho = three((lh[...], ll[...]), inverse, across)
    ortho_out[...] = ortho
    ob[...] = (ortho * 0.05).astype(BF16)
    right_y.middle()
    right_y.finish()
    index = 2 * me.x + me.c
    wide[index, :128, :] = own_right[0].astype(BF16)
    wide[index, 128:, :] = own_right[1].astype(BF16)
    gw = Gather(me, links, wide.at[index], lambda x, c: wide.at[2 * x + c])
    values = own_right[...].reshape(256, 256)
    sq[index] = jnp.broadcast_to(jnp.sum(values * values, axis=0, keepdims=True), (8, 256))
    mark = sq.at[index]
    came = [links.to(mark, mark, peer) for peer in me.tensor_peers()]
    stores = []

    def finish_block(x, c):
        cols = rows_at((2 * x + c) * 256, 256, 256)
        update = lax.dot_general(
            ob[...], wide[2 * x + c], (across, ((), ())), preferred_element_type=F32
        )
        buf[:, cols] = buf[:, cols] - update
        store = pltpu.make_async_copy(
            buf.at[:, cols], new_out.at[:, cols], local.at[4 + len(stores)]
        )
        store.start()
        stores.append(store)

    finish_block(me.x, me.c)
    gw.first()
    finish_block(me.xm, me.c)
    gw.second()
    finish_block(me.xp, me.c)
    gw.s0.wait_recv()
    finish_block(me.x, me.sib)
    gw.third()
    finish_block(me.xo, me.c)
    gw.s1.wait_recv()
    finish_block(me.xp, me.sib)
    gw.s2.wait_recv()
    finish_block(me.xm, me.sib)
    for copy in came:
        copy.wait_recv()
    squares = sq[0]
    for b in range(1, 8):
        squares += sq[b]
    q_out[...] = values * lax.rsqrt(squares[:1] + 1e-06)
    gw.s3.wait_recv()
    finish_block(me.xo, me.sib)
    for store in stores:
        store.wait()
    links.finish()


def whole_step(acts, out_grad, momentum, q_basis):
    any_space = pl.BlockSpec(memory_space=pl.ANY)
    in_vmem = pl.BlockSpec(memory_space=pltpu.VMEM)
    copies = 120
    vm = pltpu.VMEM
    scratch = [
        vm((1024, 640), BF16),
        vm((4, 640, 256), BF16),
        vm((640, 2048), F32),
        vm((8, 256, 256), F32),
        vm((2048, 256), BF16),
        vm((2048, 256), BF16),
        vm((4, 256, 256), F32),
        vm((4, 256, 256), BF16),
        vm((4, 256, 256), BF16),
        vm((4, 256, 2048), BF16),
        vm((2, 640, 128), F32),
        vm((3, 2, 160, 128), F32),
        vm((2, 160, 128), F32),
        vm((2, 160, 128), F32),
        vm((7, 40, 128), F32),
        vm((40, 128), F32),
        vm((2, 640, 128), F32),
        vm((640, 256), BF16),
        vm((640, 256), BF16),
        vm((256, 640), BF16),
        vm((256, 640), BF16),
        vm((256, 256), F32),
        vm((256, 256), F32),
        vm((4, 128, 256), F32),
        vm((2, 128, 256), F32),
        vm((256, 256), F32),
        vm((256, 256), F32),
        vm((4, 2, 256, 256), F32),
        vm((4, 256, 256), F32),
        vm((4, 2, 128, 256), F32),
        vm((3, 128, 256), F32),
        vm((128, 256), F32),
        vm((128, 256), F32),
        vm((3, 4, 32, 256), F32),
        vm((4, 32, 256), F32),
        vm((4, 32, 256), F32),
        vm((3, 32, 256), F32),
        vm((32, 256), F32),
        vm((3, 32, 256), F32),
        vm((32, 256), F32),
        vm((64, 256), F32),
        vm((7, 8, 256), F32),
        vm((8, 256), F32),
        vm((64, 256), F32),
        vm((2, 128, 256), F32),
        vm((8, 256, 256), BF16),
        vm((8, 8, 256), F32),
        vm((640, 256), BF16),
        pltpu.SemaphoreType.DMA((copies,)),
        pltpu.SemaphoreType.DMA((copies,)),
        pltpu.SemaphoreType.DMA((12,)),
    ]
    return pl.pallas_call(
        step_kernel,
        out_shape=(
            jax.ShapeDtypeStruct((640, 2048), F32),
            jax.ShapeDtypeStruct((640, 256), F32),
            jax.ShapeDtypeStruct((256, 256), F32),
        ),
        in_specs=[any_space] * 4,
        out_specs=(any_space, in_vmem, in_vmem),
        scratch_shapes=scratch,
        compiler_params=pltpu.CompilerParams(
            collective_id=0, has_side_effects=True, vmem_limit_bytes=60 * 2**20
        ),
        name="whole_step",
    )(acts, out_grad, momentum, q_basis)


def solution(mesh):
    split = Mesh(mesh.devices.reshape(4, 8, 4, 2), ("dp_0", "dp_1", "tensor_0", "tensor_1"))
    return jax.shard_map(
        whole_step,
        mesh=split,
        in_specs=(P(DP, TENSOR), P(DP_TENSOR, None), P(DP_TENSOR, None), P(TENSOR, None)),
        out_specs=(P(DP_TENSOR, None), P(TENSOR, None), P(TENSOR, None)),
        check_vma=False,
    )
```

time: 288 us -> 130 us (0.45)
  blocking collectives: 59.4 us -> 0 us
  other arithmetic: 56.2 us -> 0 us
  Pallas kernels: 66.3 us -> 122 us
  waiting for transfers between devices: 49.6 us -> 0 us
  matrix products: 25.5 us -> 0 us
  starting transfers between devices: 14.9 us -> 0 us
  local copies, waits for them, and re-layouts: 12.8 us -> 7.11 us
    all_to_all x3 -> x0, blocking collectives: 59.4 us -> none  [the longest x1 29.8 us: summed_on_arrival(): lax.all_to_all(blocks, axis, split_axis=0, concat_axis=0, tiled=True)]
    pallas_call x1, Pallas kernels: 66.3 us -> 122 us  [whole_step(): pl.pallas_call(step_kernel, out_shape=(jax.ShapeDtypeStruct((640, 2048),...]
    another operation x10 -> x0, other arithmetic: 54.8 us -> none  [the longest x6 33.9 us: orthonormal(): chol = jnp.linalg.cholesky(gram)]
    all_to_all x2 -> x0, waiting for transfers between devices: 49.6 us -> none  [from_everyone(): return lax.all_to_all(copies, axis, split_axis=0, concat_axis=0, tiled=True)]
    dot_general x3 -> x0, matrix products: 23.4 us -> none  [the longest x1 11.8 us: body(): jnp.dot(ortho, right.T, precision=HIGH, preferred_element_type=jnp.float32)]
    all_to_all x2 -> x0, starting transfers between devices: 14.9 us -> none  [from_everyone(): return lax.all_to_all(copies, axis, split_axis=0, concat_axis=0, tiled=True)]
    another operation x10 -> x0, local copies, waits for them, and re-layouts: 4.22 us -> none
    broadcast_in_dim x3 -> x0, local copies, waits for them, and re-layouts: 3.02 us -> none  [from_everyone(): copies = jnp.broadcast_to(value, (lax.axis_size(axis), *value.shape))]
  transfers between devices with their start and end apart: 2 -> 0, of which waited for: 2 -> 0; matrix products, arithmetic and copies ran while one was open for 1% -> 0% of each run, Pallas kernels for 0% -> 0%
where the time goes in v2:
time: 130 us
  Pallas kernels  122 us (94%)
  local copies, waits for them, and re-layouts  7.11 us (5%)
    pallas_call x1, Pallas kernels, whole_step(): pl.pallas_call(step_kernel, out_shape=(jax.ShapeDtypeStruct((640, 2048),...  122 us
    unnamed x7, local copies, waits for them, and re-layouts  7.11 us

profile of v2, /device:TPU:1, one launch (start us, length us, event | category | flops | bytes accessed | tf_op | source)
XLA Modules:
  0.0 129.8 jit_solution(13604743930457661744)
XLA Ops:
  0.6 122.0 %whole_step.1 = (f32[640,2048]{1,0:T(8,128)}, f32[640,256]{1,0:T(8,128)}, f32[256,256]{1,0:T(8,128)}) custom-call(bf16[1024,640]{1,0:T(8,128)(2,1)} %acts.1, bf16[128,2048]{1,0:T(8,128)(2,1)} %og.1, f32[640,2048]{1,0:T(8,128)} %mom.1, f32[256,256]{1,0:T(8,128)} %q.1), custom_call_target="tpu_custom_call" | custom-call | tf_op jit(solution)/shard_map/whole_step/pallas_call | solution.py:516
  122.6 0.0 copy-start
  122.6 0.0 copy-start.1
  122.7 5.6 %copy.10 = f32[640,2048]{1,0:T(8,128)} copy(f32[640,2048]{1,0:T(8,128)} %get-tuple-element.6) | data formatting | bytes 10485760
  128.2 0.0 copy-done
  128.2 0.8 copy.11
  129.1 0.0 copy-done.1
  129.1 0.7 copy.12
Async XLA Ops:
  122.6 5.6 %copy-start = (f32[640,256]{1,0:T(8,128)S(1)}, f32[640,256]{1,0:T(8,128)}, u32[]{:S(2)}) copy-start(f32[640,256]{1,0:T(8,128)} %get-tuple-element.7) | copy-start | bytes 1966084
  122.6 6.4 %copy-start.1 = (f32[256,256]{1,0:T(8,128)S(1)}, f32[256,256]{1,0:T(8,128)}, u32[]{:S(2)}) copy-start(f32[256,256]{1,0:T(8,128)} %get-tuple-element.8) | copy-start | bytes 786436

commit v3 on v2

--- a/solution.py
+++ b/solution.py
@@ -34,11 +34,11 @@
         self.xo, self.yo = lax.rem(self.x + 2, 4), lax.rem(self.y + 2, 4)
 
     def tensor_peers(self):
-        peers = [{"tensor_1": self.sib}]
+        peers = [({"tensor_1": self.sib}, 2 * self.x + self.sib)]
         for n in range(1, 4):
             there = lax.rem(self.x + n, 4)
-            peers.append({"tensor_0": there, "tensor_1": self.c})
-            peers.append({"tensor_0": there, "tensor_1": self.sib})
+            for core in (self.c, self.sib):
+                peers.append(({"tensor_0": there, "tensor_1": core}, 2 * there + core))
         return peers
 
     def zk(self, k):
@@ -47,7 +47,7 @@
 
 def greet(me):
     barrier = pltpu.get_barrier_semaphore()
-    targets = me.tensor_peers()
+    targets = [peer for peer, _ in me.tensor_peers()]
     targets += [{"dp_0": me.yp}, {"dp_0": me.ym}]
     targets += [{"dp_1": me.zk(k)} for k in range(1, 8)]
     for target in targets:
@@ -201,12 +201,12 @@
 
 
 def step_kernel(
-    acts, og, mom, q, new_out, ortho_out, q_out,
-    actsv, acts_t, buf, qg, qh, ql, yg, yh, yl, ogg,
+    acts, og, mom, q, buf_out, ob, wide_out, ortho_out, q_out,
+    actsv, acts_t, buf, qg, qh, ql, yg, yh, yl, ogg, y_own,
     part, r_left, s1, chunk, zr, zs, full,
-    lh, ll, lth, ltl, gram, gram_r, gram_x, gram_f, a, inv,
+    bth, btl, lh, ll, gram, gram_r, gram_s, a, inv,
     cc, c_sib, c_sum, rx, sx, tx, ry, sy, ty, rxy, sxy, ryx, syx,
-    rest, zr2, zs2, all_z, own_right, wide, sq, ob,
+    rest, zr2, zs2, all_z, own_right, wide, sq,
     send, recv, local,
 ):
     me = Place()
@@ -227,37 +227,52 @@
     loads[2].wait()
     for j in range(4):
         acts_t[j] = actsv[256 * j : 256 * (j + 1), :].T
+    loads[0].wait()
+    loads[1].wait()
+    loads[3].wait()
+    own = ogg.at[me.x, own_rows]
+
+    def og_times(b, first=False):
+        high, low = halves(qg[b])
+        qh[b], ql[b] = high, low
+        lhs = own[:, rows_at(b * 256, 256, 256)]
+        share = mxu(lhs, high) + mxu(lhs, low)
+        y_own[...] = share if first else y_own[...] + share
+
+    def momentum_times(b, first=False):
+        @pl.loop(0, 5)
+        def _(t):
+            rows = rows_at(t * 128, 128)
+            share = three(halves(buf[rows, rows_at(b * 256, 256, 256)]), (qh[b], ql[b]))
+            for half in range(2):
+                piece = share[:, 128 * half : 128 * half + 128]
+                part[half, rows, :] = piece if first else part[half, rows, :] + piece
+
+    def take(x, c, first=False):
+        og_times(2 * x + c, first)
+        momentum_times(2 * x + c, first)
+
+    take(me.x, me.c, True)
     gq.first()
     gq.second()
+    gq.s0.wait_recv()
+    take(me.x, me.sib)
+    take(me.xm, me.c)
+    take(me.xp, me.c)
+    gq.s1.wait_recv()
+    take(me.xp, me.sib)
+    gq.s2.wait_recv()
+    take(me.xm, me.sib)
     gq.third()
-    loads[0].wait()
-    gq.rest()
-
-    @pl.loop(0, 8)
-    def _(b):
-        high, low = halves(qg[b])
-        rows = pl.ds(pl.multiple_of(b * 256, 256), 256)
-        qh[rows], ql[rows] = high, low
-
-    loads[1].wait()
-    own = ogg[me.x, own_rows, :]
+    take(me.xo, me.c)
+    gq.s3.wait_recv()
+    og_times(2 * me.xo + me.sib)
+    yg[me.x, own_rows, :] = y_own[...]
     own_y = yg.at[me.x, own_rows]
-    yg[me.x, own_rows, :] = mxu(own, qh[...]) + mxu(own, ql[...])
     gy = Gather(me, links, own_y, lambda x, c: yg.at[x, pl.ds(pl.multiple_of(c * 128, 128), 128)])
-    loads[3].wait()
-
-    def momentum_part(t):
-        rows = pl.ds(pl.multiple_of(t * 128, 128), 128)
-        high, low = halves(buf[rows, :])
-        acc = mxu(high, qh[...]) + mxu(high, ql[...]) + mxu(low, qh[...])
-        acc = acc * (0.95 / 32)
-        part[0, rows, :] = acc[:, :128]
-        part[1, rows, :] = acc[:, 128:]
-
-    pl.loop(0, 2)(momentum_part)
+    momentum_times(2 * me.xo + me.sib)
     gy.first()
     gy.second()
-    pl.loop(2, 5)(momentum_part)
     gy.third()
     gy.rest()
     go = Gather(
@@ -274,9 +289,9 @@
         for j in range(4):
             lhs = acts_t[j, rows, :]
             acc += mxu(lhs, yh[j]) + mxu(lhs, yl[j])
-        acc = acc * (1 / 32)
-        part[0, rows, :] += acc[:, :128]
-        part[1, rows, :] += acc[:, 128:]
+        for half in range(2):
+            piece = acc[:, 128 * half : 128 * half + 128]
+            part[half, rows, :] = (0.95 * part[half, rows, :] + piece) * (1 / 32)
 
     def of_y(ref, y):
         return ref.at[:, pl.ds(pl.multiple_of(y * 160, 32), 160)]
@@ -307,64 +322,83 @@
     spot = full.at[half, pl.ds(pl.multiple_of(me.y * 160 + row, 8), 40)]
     came = [links.to(zs, spot, {"dp_1": me.zk(k)}) for k in range(1, 8)]
     spot[...] = total
-    for copy in came:
-        copy.wait_recv()
-    spread = RingSpread(links, "dp_0", ys, lambda y: of_y(full, y))
     go.third()
-    spread.middle()
     go.rest()
 
     @pl.loop(0, 8)
     def _(n):
-        cols = pl.ds(pl.multiple_of(n * 256, 256), 256)
+        cols = rows_at(n * 256, 256, 256)
         acc = 0.95 * buf[:, cols]
         for j in range(4):
             acc += mxu(acts_t[j], ogg[j, :, cols])
         buf[:, cols] = acc
-
-    spread.finish()
-    for half in range(2):
-        cols = slice(128 * half, 128 * half + 128)
-        lh[:, cols], ll[:, cols] = halves(full[half])
-        lth[cols, :], ltl[cols, :] = halves(full[half].T)
-
-    gram[...] = three((lth[...], ltl[...]), (lh[...], ll[...]))
-    pair = links.to(gram, gram_r, {"tensor_1": me.sib})
-
-    def product_with(core):
+        for j in range(4):
+            bth[j, cols, :], btl[j, cols, :] = halves(acc[160 * j : 160 * j + 160].T)
+
+    store = pltpu.make_async_copy(buf, buf_out, local.at[4])
+    store.start()
+    for copy in came:
+        copy.wait_recv()
+
+    def take_left(j, first=False):
+        chunk_rows = rows_at(j * 160, 160, 32)
+        rows = jnp.concatenate([full[0, chunk_rows, :], full[1, chunk_rows, :]], axis=1)
+        pair = halves(rows)
+        lh[j], ll[j] = pair
+        share = three(halves(rows.T), pair)
+        gram[...] = share if first else gram[...] + share
+
+    def product_with(core, j, first=False):
         @pl.loop(0, 4)
         def _(n):
             cols = rows_at((2 * n + core) * 256, 256, 256)
-            block = three((lth[...], ltl[...]), halves(buf[:, cols]))
-            cc[n, core] = block.T
-
-    product_with(me.sib)
+            share = three((bth[j, cols, :], btl[j, cols, :]), (lh[j], ll[j]))
+            cc[n, core] = share if first else cc[n, core] + share
+
+    spread = RingSpread(links, "dp_0", ys, lambda y: of_y(full, y))
+    take_left(me.y, True)
+    product_with(me.sib, me.y, True)
+    spread.middle()
+    product_with(me.c, me.y, True)
+    take_left(me.ym)
+    spread.down.wait_recv()
+    take_left(me.yp)
+    for core in (me.sib, me.c):
+        product_with(core, me.ym)
+        product_with(core, me.yp)
+    spread.far.wait_recv()
+    take_left(me.yo)
+    index = 2 * me.x + me.c
+    gram_in = []
+    for peer, there in me.tensor_peers():
+        gram_in.append(links.to(gram.at[rows_at(there * 32, 32)], gram_r.at[index], peer))
+    gram_r[index] = gram[rows_at(index * 32, 32), :]
+    product_with(me.sib, me.yo)
     swap = links.to(cc.at[:, me.sib], c_sib, {"tensor_1": me.sib})
-    pair.wait_recv()
-    half_rows = rows_at(me.c * 128, 128)
-    gram_x[me.x] = gram[half_rows, :] + gram_r[half_rows, :]
-    gram_spread = RingSpread(links, "tensor_0", xs, lambda x: gram_x.at[x])
-    product_with(me.c)
-    gram_spread.middle()
+    for copy in gram_in:
+        copy.wait_recv()
+    total = gram_r[0]
+    for b in range(1, 8):
+        total += gram_r[b]
+    gram_s[...] = total
+    gram_rows = a.at[rows_at(index * 32, 32)]
+    gram_in = [links.to(gram_s, gram_rows, peer) for peer, _ in me.tensor_peers()]
+    gram_rows[...] = total
+    product_with(me.c, me.yo)
     swap.wait_recv()
     c_sum[...] = cc[:, me.c].reshape(4, 2, 128, 256) + c_sib[...].reshape(4, 2, 128, 256)
     x_first = RingSum(links, "tensor_0", xs, lambda x: c_sum.at[x, 0], rx, sx)
     y_first = RingSum(
         links, "dp_0", ys, lambda y: c_sum.at[:, 1, rows_at(y * 32, 32)], ry, sy
     )
-    gram_spread.finish()
-    gram_f[me.c] = ((gram_x[0] + gram_x[1]) + gram_x[2]) + gram_x[3]
-    here = gram_f.at[me.c]
-    whole = links.to(here, here, {"tensor_1": me.sib})
     same = lax.broadcasted_iota(jnp.int32, (256, 256), 0) == lax.broadcasted_iota(
         jnp.int32, (256, 256), 1
     )
     inv[...] = jnp.where(same, 1.0, 0.0).astype(F32)
     y_first.middle()
     x_first.middle()
-    whole.wait_recv()
-    a[:128, :] = gram_f[0]
-    a[128:, :] = gram_f[1]
+    for copy in gram_in:
+        copy.wait_recv()
 
     factor_block(0, a, inv)
     tx[...] = x_first.total()
@@ -402,61 +436,73 @@
     right_y = RingSpread(
         links, "dp_0", ys, lambda y: own_right.at[:, rows_at(y * 32, 32)]
     )
-    ortho = three((lh[...], ll[...]), inverse, across)
+    ortho = three((lh[...].reshape(640, 256), ll[...].reshape(640, 256)), inverse, across)
     ortho_out[...] = ortho
     ob[...] = (ortho * 0.05).astype(BF16)
     right_y.middle()
     right_y.finish()
-    index = 2 * me.x + me.c
     wide[index, :128, :] = own_right[0].astype(BF16)
     wide[index, 128:, :] = own_right[1].astype(BF16)
     gw = Gather(me, links, wide.at[index], lambda x, c: wide.at[2 * x + c])
     values = own_right[...].reshape(256, 256)
     sq[index] = jnp.broadcast_to(jnp.sum(values * values, axis=0, keepdims=True), (8, 256))
     mark = sq.at[index]
-    came = [links.to(mark, mark, peer) for peer in me.tensor_peers()]
-    stores = []
-
-    def finish_block(x, c):
-        cols = rows_at((2 * x + c) * 256, 256, 256)
-        update = lax.dot_general(
-            ob[...], wide[2 * x + c], (across, ((), ())), preferred_element_type=F32
-        )
-        buf[:, cols] = buf[:, cols] - update
-        store = pltpu.make_async_copy(
-            buf.at[:, cols], new_out.at[:, cols], local.at[4 + len(stores)]
-        )
-        store.start()
-        stores.append(store)
-
-    finish_block(me.x, me.c)
+    came = [links.to(mark, mark, peer) for peer, _ in me.tensor_peers()]
     gw.first()
-    finish_block(me.xm, me.c)
     gw.second()
-    finish_block(me.xp, me.c)
-    gw.s0.wait_recv()
-    finish_block(me.x, me.sib)
-    gw.third()
-    finish_block(me.xo, me.c)
-    gw.s1.wait_recv()
-    finish_block(me.xp, me.sib)
-    gw.s2.wait_recv()
-    finish_block(me.xm, me.sib)
     for copy in came:
         copy.wait_recv()
     squares = sq[0]
     for b in range(1, 8):
         squares += sq[b]
     q_out[...] = values * lax.rsqrt(squares[:1] + 1e-06)
-    gw.s3.wait_recv()
-    finish_block(me.xo, me.sib)
-    for store in stores:
-        store.wait()
+    gw.third()
+    gw.rest()
+    wide_out[...] = wide[...]
+    store.wait()
     links.finish()
+
+
+def apply_kernel(buf, ob, wide, ortho, q, new_out, ortho_out, q_out):
+    lhs = ob[...]
+    for b in range(8):
+        cols = slice(256 * b, 256 * b + 256)
+        update = lax.dot_general(
+            lhs, wide[b], (((1,), (1,)), ((), ())), preferred_element_type=F32
+        )
+        new_out[:, cols] = buf[:, cols] - update
+    ortho_out[...] = ortho[...]
+    q_out[...] = q[...]
+
+
+def apply_update(buf, ob, wide, ortho, q):
+    def tile(rows, cols):
+        return pl.BlockSpec((rows, cols), lambda i: (i, 0))
+
+    return pl.pallas_call(
+        apply_kernel,
+        grid=(4,),
+        out_shape=(
+            jax.ShapeDtypeStruct((640, 2048), F32),
+            jax.ShapeDtypeStruct((640, 256), F32),
+            jax.ShapeDtypeStruct((256, 256), F32),
+        ),
+        in_specs=[
+            tile(160, 2048),
+            tile(160, 256),
+            pl.BlockSpec((8, 256, 256), lambda i: (0, 0, 0)),
+            tile(160, 256),
+            tile(64, 256),
+        ],
+        out_specs=(tile(160, 2048), tile(160, 256), tile(64, 256)),
+        compiler_params=pltpu.CompilerParams(vmem_limit_bytes=56 * 2**20),
+        name="apply_update",
+    )(buf, ob, wide, ortho, q)
 
 
 def whole_step(acts, out_grad, momentum, q_basis):
     any_space = pl.BlockSpec(memory_space=pl.ANY)
+    in_hbm = pl.BlockSpec(memory_space=pltpu.HBM)
     in_vmem = pl.BlockSpec(memory_space=pltpu.VMEM)
     copies = 120
     vm = pltpu.VMEM
@@ -465,12 +511,13 @@
         vm((4, 640, 256), BF16),
         vm((640, 2048), F32),
         vm((8, 256, 256), F32),
-        vm((2048, 256), BF16),
-        vm((2048, 256), BF16),
+        vm((8, 256, 256), BF16),
+        vm((8, 256, 256), BF16),
         vm((4, 256, 256), F32),
         vm((4, 256, 256), BF16),
         vm((4, 256, 256), BF16),
         vm((4, 256, 2048), BF16),
+        vm((128, 256), F32),
         vm((2, 640, 128), F32),
         vm((3, 2, 160, 128), F32),
         vm((2, 160, 128), F32),
@@ -478,14 +525,13 @@
         vm((7, 40, 128), F32),
         vm((40, 128), F32),
         vm((2, 640, 128), F32),
-        vm((640, 256), BF16),
-        vm((640, 256), BF16),
-        vm((256, 640), BF16),
-        vm((256, 640), BF16),
+        vm((4, 2048, 160), BF16),
+        vm((4, 2048, 160), BF16),
+        vm((4, 160, 256), BF16),
+        vm((4, 160, 256), BF16),
         vm((256, 256), F32),
-        vm((256, 256), F32),
-        vm((4, 128, 256), F32),
-        vm((2, 128, 256), F32),
+        vm((8, 32, 256), F32),
+        vm((32, 256), F32),
         vm((256, 256), F32),
         vm((256, 256), F32),
         vm((4, 2, 256, 256), F32),
@@ -508,26 +554,28 @@
         vm((2, 128, 256), F32),
         vm((8, 256, 256), BF16),
         vm((8, 8, 256), F32),
-        vm((640, 256), BF16),
         pltpu.SemaphoreType.DMA((copies,)),
         pltpu.SemaphoreType.DMA((copies,)),
         pltpu.SemaphoreType.DMA((12,)),
     ]
-    return pl.pallas_call(
+    outs = pl.pallas_call(
         step_kernel,
         out_shape=(
             jax.ShapeDtypeStruct((640, 2048), F32),
+            jax.ShapeDtypeStruct((640, 256), BF16),
+            jax.ShapeDtypeStruct((8, 256, 256), BF16),
             jax.ShapeDtypeStruct((640, 256), F32),
             jax.ShapeDtypeStruct((256, 256), F32),
         ),
-        in_specs=[any_space] * 4,
-        out_specs=(any_space, in_vmem, in_vmem),
+        in_specs=[in_hbm] * 4,
+        out_specs=(any_space, in_vmem, in_vmem, in_vmem, in_vmem),
         scratch_shapes=scratch,
         compiler_params=pltpu.CompilerParams(
             collective_id=0, has_side_effects=True, vmem_limit_bytes=60 * 2**20
         ),
         name="whole_step",
     )(acts, out_grad, momentum, q_basis)
+    return apply_update(*outs)
 
 
 def solution(mesh):

time: 130 us -> 138 us (1.062)
  Pallas kernels: 122 us -> 138 us
  local copies, waits for them, and re-layouts: 7.11 us -> 0 us
    pallas_call x1, Pallas kernels: 122 us -> 130 us  [whole_step(): pl.pallas_call(step_kernel, out_shape=(jax.ShapeDtypeStruct((640, 2048),...]
    pallas_call x0 -> x1, Pallas kernels: none -> 7.18 us  [apply_update(): pl.pallas_call(apply_kernel, grid=(4,), out_shape=(jax.ShapeDtypeStruct((...]
    unnamed x7 -> x0, local copies, waits for them, and re-layouts: 7.11 us -> none
where the time goes in v3:
time: 138 us
  Pallas kernels  138 us (100%)
    pallas_call x1, Pallas kernels, whole_step(): pl.pallas_call(step_kernel, out_shape=(jax.ShapeDtypeStruct((640, 2048),...  130 us
    pallas_call x1, Pallas kernels, apply_update(): pl.pallas_call(apply_kernel, grid=(4,), out_shape=(jax.ShapeDtypeStruct((...  7.18 us

profile of v3, /device:TPU:1, one launch (start us, length us, event | category | flops | bytes accessed | tf_op | source)
XLA Modules:
  0.0 138.1 jit_solution(12225228694403445487)
XLA Ops:
  0.6 130.3 %whole_step.1 = (f32[640,2048]{1,0:T(8,128)}, bf16[640,256]{1,0:T(8,128)(2,1)}, bf16[8,256,256]{2,1,0:T(8,128)(2,1)}, f32[640,256]{1,0:T(8,128)}, f32[256,256]{1,0:T(8,128)}) custom-call(bf16[1024,640]{1,0:T(8,128)(2,1)} %acts.1, bf16[128,2048]{1,0:T(8,128)(2,1)} %og.1, f32[640,2048]{1,0:T(8,128)} %mom.1, f32[256,256]{1,0:T(8,128)} %q.1), custom_call_target="tpu_custom_call" | custom-call | tf_op jit(solution)/shard_map/whole_step/pallas_call | solution.py:561
  131.0 7.2 %apply_update.1 = (f32[640,2048]{1,0:T(8,128)}, f32[640,256]{1,0:T(8,128)}, f32[256,256]{1,0:T(8,128)}) custom-call(f32[640,2048]{1,0:T(8,128)} %get-tuple-element.8.buf, bf16[640,256]{1,0:T(8,128)(2,1)} %get-tuple-element.9.ob, bf16[8,256,256]{2,1,0:T(8,128)(2,1)} %get-tuple-element.10.wide, f32[640,256]{1,0:T(8,128)} %get-tuple-element.11.ortho, ...), custom_call_target="tpu_custom_call" | custom-call | tf_op jit(solution)/shard_map/apply_update/pallas_call | solution.py:482

commit v4 on v3

--- a/solution.py
+++ b/solution.py
@@ -166,7 +166,7 @@
             cols = [jnp.broadcast_to(e[:, j : j + 1], (64, 128)) for j in range(first, first + 8)]
             for n, col in enumerate(cols):
                 j = first + n
-                weight = pl.reciprocal(col[j : j + 1])
+                weight = pltpu.reciprocal(col[j : j + 1])
                 factor = jnp.where((row > j) & (row < live), col, 0.0) * weight
                 e = e - factor * e[j : j + 1]
                 for m in range(n + 1, 8):
@@ -224,6 +224,8 @@
         load.start()
     greet(me)
     gq = Gather(me, links, q, lambda x, c: qg.at[x * 2 + c])
+    gq.first()
+    gq.second()
     loads[2].wait()
     for j in range(4):
         acts_t[j] = actsv[256 * j : 256 * (j + 1), :].T
@@ -232,47 +234,42 @@
     loads[3].wait()
     own = ogg.at[me.x, own_rows]
 
-    def og_times(b, first=False):
+    def take(x, c, first=False):
+        b = 2 * x + c
+        rows = rows_at(b * 256, 256, 256)
         high, low = halves(qg[b])
-        qh[b], ql[b] = high, low
-        lhs = own[:, rows_at(b * 256, 256, 256)]
+        qh[rows, :], ql[rows, :] = high, low
+        lhs = own[:, rows]
         share = mxu(lhs, high) + mxu(lhs, low)
         y_own[...] = share if first else y_own[...] + share
 
-    def momentum_times(b, first=False):
-        @pl.loop(0, 5)
-        def _(t):
-            rows = rows_at(t * 128, 128)
-            share = three(halves(buf[rows, rows_at(b * 256, 256, 256)]), (qh[b], ql[b]))
-            for half in range(2):
-                piece = share[:, 128 * half : 128 * half + 128]
-                part[half, rows, :] = piece if first else part[half, rows, :] + piece
-
-    def take(x, c, first=False):
-        og_times(2 * x + c, first)
-        momentum_times(2 * x + c, first)
-
     take(me.x, me.c, True)
-    gq.first()
-    gq.second()
+    take(me.xm, me.c)
+    take(me.xp, me.c)
     gq.s0.wait_recv()
     take(me.x, me.sib)
-    take(me.xm, me.c)
-    take(me.xp, me.c)
+    gq.third()
+    take(me.xo, me.c)
     gq.s1.wait_recv()
     take(me.xp, me.sib)
     gq.s2.wait_recv()
     take(me.xm, me.sib)
-    gq.third()
-    take(me.xo, me.c)
     gq.s3.wait_recv()
-    og_times(2 * me.xo + me.sib)
+    take(me.xo, me.sib)
     yg[me.x, own_rows, :] = y_own[...]
     own_y = yg.at[me.x, own_rows]
     gy = Gather(me, links, own_y, lambda x, c: yg.at[x, pl.ds(pl.multiple_of(c * 128, 128), 128)])
-    momentum_times(2 * me.xo + me.sib)
+
+    def momentum_part(t):
+        rows = rows_at(t * 128, 128)
+        share = three(halves(buf[rows, :]), (qh[...], ql[...]))
+        for half in range(2):
+            part[half, rows, :] = share[:, 128 * half : 128 * half + 128]
+
+    pl.loop(0, 3)(momentum_part)
     gy.first()
     gy.second()
+    pl.loop(3, 5)(momentum_part)
     gy.third()
     gy.rest()
     go = Gather(
@@ -323,57 +320,45 @@
     came = [links.to(zs, spot, {"dp_1": me.zk(k)}) for k in range(1, 8)]
     spot[...] = total
     go.third()
-    go.rest()
-
-    @pl.loop(0, 8)
-    def _(n):
+    for copy in came:
+        copy.wait_recv()
+    spread = RingSpread(links, "dp_0", ys, lambda y: of_y(full, y))
+
+    def buffer_part(n):
         cols = rows_at(n * 256, 256, 256)
         acc = 0.95 * buf[:, cols]
         for j in range(4):
             acc += mxu(acts_t[j], ogg[j, :, cols])
         buf[:, cols] = acc
-        for j in range(4):
-            bth[j, cols, :], btl[j, cols, :] = halves(acc[160 * j : 160 * j + 160].T)
-
+        bth[cols, :], btl[cols, :] = halves(acc.T)
+
+    go.rest()
+    pl.loop(0, 4)(buffer_part)
+    spread.middle()
+    pl.loop(4, 8)(buffer_part)
     store = pltpu.make_async_copy(buf, buf_out, local.at[4])
     store.start()
-    for copy in came:
-        copy.wait_recv()
-
-    def take_left(j, first=False):
-        chunk_rows = rows_at(j * 160, 160, 32)
-        rows = jnp.concatenate([full[0, chunk_rows, :], full[1, chunk_rows, :]], axis=1)
-        pair = halves(rows)
-        lh[j], ll[j] = pair
-        share = three(halves(rows.T), pair)
-        gram[...] = share if first else gram[...] + share
-
-    def product_with(core, j, first=False):
+    spread.finish()
+    lt = []
+    for half in range(2):
+        cols = slice(128 * half, 128 * half + 128)
+        lh[:, cols], ll[:, cols] = halves(full[half])
+        lt.append(full[half].T)
+    left = lh[...], ll[...]
+    gram[...] = three(halves(jnp.concatenate(lt, axis=0)), left)
+
+    def product_with(core):
         @pl.loop(0, 4)
         def _(n):
-            cols = rows_at((2 * n + core) * 256, 256, 256)
-            share = three((bth[j, cols, :], btl[j, cols, :]), (lh[j], ll[j]))
-            cc[n, core] = share if first else cc[n, core] + share
-
-    spread = RingSpread(links, "dp_0", ys, lambda y: of_y(full, y))
-    take_left(me.y, True)
-    product_with(me.sib, me.y, True)
-    spread.middle()
-    product_with(me.c, me.y, True)
-    take_left(me.ym)
-    spread.down.wait_recv()
-    take_left(me.yp)
-    for core in (me.sib, me.c):
-        product_with(core, me.ym)
-        product_with(core, me.yp)
-    spread.far.wait_recv()
-    take_left(me.yo)
+            rows = rows_at((2 * n + core) * 256, 256, 256)
+            cc[n, core] = three((bth[rows, :], btl[rows, :]), (lh[...], ll[...]))
+
     index = 2 * me.x + me.c
     gram_in = []
     for peer, there in me.tensor_peers():
         gram_in.append(links.to(gram.at[rows_at(there * 32, 32)], gram_r.at[index], peer))
     gram_r[index] = gram[rows_at(index * 32, 32), :]
-    product_with(me.sib, me.yo)
+    product_with(me.sib)
     swap = links.to(cc.at[:, me.sib], c_sib, {"tensor_1": me.sib})
     for copy in gram_in:
         copy.wait_recv()
@@ -384,7 +369,7 @@
     gram_rows = a.at[rows_at(index * 32, 32)]
     gram_in = [links.to(gram_s, gram_rows, peer) for peer, _ in me.tensor_peers()]
     gram_rows[...] = total
-    product_with(me.c, me.yo)
+    product_with(me.c)
     swap.wait_recv()
     c_sum[...] = cc[:, me.c].reshape(4, 2, 128, 256) + c_sib[...].reshape(4, 2, 128, 256)
     x_first = RingSum(links, "tensor_0", xs, lambda x: c_sum.at[x, 0], rx, sx)
@@ -436,7 +421,7 @@
     right_y = RingSpread(
         links, "dp_0", ys, lambda y: own_right.at[:, rows_at(y * 32, 32)]
     )
-    ortho = three((lh[...].reshape(640, 256), ll[...].reshape(640, 256)), inverse, across)
+    ortho = three((lh[...], ll[...]), inverse, across)
     ortho_out[...] = ortho
     ob[...] = (ortho * 0.05).astype(BF16)
     right_y.middle()
@@ -481,20 +466,20 @@
 
     return pl.pallas_call(
         apply_kernel,
-        grid=(4,),
+        grid=(8,),
         out_shape=(
             jax.ShapeDtypeStruct((640, 2048), F32),
             jax.ShapeDtypeStruct((640, 256), F32),
             jax.ShapeDtypeStruct((256, 256), F32),
         ),
         in_specs=[
-            tile(160, 2048),
-            tile(160, 256),
+            tile(80, 2048),
+            tile(80, 256),
             pl.BlockSpec((8, 256, 256), lambda i: (0, 0, 0)),
-            tile(160, 256),
-            tile(64, 256),
+            tile(80, 256),
+            tile(32, 256),
         ],
-        out_specs=(tile(160, 2048), tile(160, 256), tile(64, 256)),
+        out_specs=(tile(80, 2048), tile(80, 256), tile(32, 256)),
         compiler_params=pltpu.CompilerParams(vmem_limit_bytes=56 * 2**20),
         name="apply_update",
     )(buf, ob, wide, ortho, q)
@@ -511,8 +496,8 @@
         vm((4, 640, 256), BF16),
         vm((640, 2048), F32),
         vm((8, 256, 256), F32),
-        vm((8, 256, 256), BF16),
-        vm((8, 256, 256), BF16),
+        vm((2048, 256), BF16),
+        vm((2048, 256), BF16),
         vm((4, 256, 256), F32),
         vm((4, 256, 256), BF16),
         vm((4, 256, 256), BF16),
@@ -525,10 +510,10 @@
         vm((7, 40, 128), F32),
         vm((40, 128), F32),
         vm((2, 640, 128), F32),
-        vm((4, 2048, 160), BF16),
-        vm((4, 2048, 160), BF16),
-        vm((4, 160, 256), BF16),
-        vm((4, 160, 256), BF16),
+        vm((2048, 640), BF16),
+        vm((2048, 640), BF16),
+        vm((640, 256), BF16),
+        vm((640, 256), BF16),
         vm((256, 256), F32),
         vm((8, 32, 256), F32),
         vm((32, 256), F32),

time: 138 us -> 132 us (0.957)
  Pallas kernels: 138 us -> 131 us
    pallas_call x1, Pallas kernels: 130 us -> 122 us  [whole_step(): pl.pallas_call(step_kernel, out_shape=(jax.ShapeDtypeStruct((640, 2048),...]
    pallas_call x1, Pallas kernels: 7.18 us -> 9.24 us  [apply_update(): pl.pallas_call(apply_kernel, grid=(8,), out_shape=(jax.ShapeDtypeStruct((...]
where the time goes in v4:
time: 132 us; the launch traced here: 131 us
  Pallas kernels  131 us (99%)
    pallas_call x1, Pallas kernels, whole_step(): pl.pallas_call(step_kernel, out_shape=(jax.ShapeDtypeStruct((640, 2048),...  122 us
    pallas_call x1, Pallas kernels, apply_update(): pl.pallas_call(apply_kernel, grid=(8,), out_shape=(jax.ShapeDtypeStruct((...  9.24 us

profile of v4, /device:TPU:1, one launch (start us, length us, event | category | flops | bytes accessed | tf_op | source)
XLA Modules:
  0.0 131.4 jit_solution(593965340192043495)
XLA Ops:
  0.6 121.5 %whole_step.1 = (f32[640,2048]{1,0:T(8,128)}, bf16[640,256]{1,0:T(8,128)(2,1)}, bf16[8,256,256]{2,1,0:T(8,128)(2,1)}, f32[640,256]{1,0:T(8,128)}, f32[256,256]{1,0:T(8,128)}) custom-call(bf16[1024,640]{1,0:T(8,128)(2,1)} %acts.1, bf16[128,2048]{1,0:T(8,128)(2,1)} %og.1, f32[640,2048]{1,0:T(8,128)} %mom.1, f32[256,256]{1,0:T(8,128)} %q.1), custom_call_target="tpu_custom_call" | custom-call | tf_op jit(solution)/shard_map/whole_step/pallas_call | solution.py:546
  122.2 9.2 %apply_update.1 = (f32[640,2048]{1,0:T(8,128)}, f32[640,256]{1,0:T(8,128)}, f32[256,256]{1,0:T(8,128)}) custom-call(f32[640,2048]{1,0:T(8,128)} %get-tuple-element.8.buf, bf16[640,256]{1,0:T(8,128)(2,1)} %get-tuple-element.9.ob, bf16[8,256,256]{2,1,0:T(8,128)(2,1)} %get-tuple-element.10.wide, f32[640,256]{1,0:T(8,128)} %get-tuple-element.11.ortho, ...), custom_call_target="tpu_custom_call" | custom-call | tf_op jit(solution)/shard_map/apply_update/pallas_call | solution.py:467

commit v5 on v4

--- a/solution.py
+++ b/solution.py
@@ -48,7 +48,7 @@
 def greet(me):
     barrier = pltpu.get_barrier_semaphore()
     targets = [peer for peer, _ in me.tensor_peers()]
-    targets += [{"dp_0": me.yp}, {"dp_0": me.ym}]
+    targets += [{"dp_0": me.yp}, {"dp_0": me.ym}, {"dp_0": me.yo}]
     targets += [{"dp_1": me.zk(k)} for k in range(1, 8)]
     for target in targets:
         pl.semaphore_signal(barrier, inc=1, device_id=target, device_id_type=MESH)
@@ -144,6 +144,20 @@
     def finish(self):
         self.down.wait_recv()
         self.far.wait_recv()
+
+
+class DirectSum:
+    def __init__(self, links, axis, places, src, came):
+        own, *others = places
+        self.mine, self.came = src(own), came
+        self.copies = [
+            links.to(src(there), came.at[n], {axis: there}) for n, there in enumerate(others)
+        ]
+
+    def total(self):
+        for copy in self.copies:
+            copy.wait_recv()
+        return self.mine[...] + self.came[0] + self.came[1] + self.came[2]
 
 
 def three(a, b, dims=((1,), (0,))):
@@ -205,7 +219,7 @@
     actsv, acts_t, buf, qg, qh, ql, yg, yh, yl, ogg, y_own,
     part, r_left, s1, chunk, zr, zs, full,
     bth, btl, lh, ll, gram, gram_r, gram_s, a, inv,
-    cc, c_sib, c_sum, rx, sx, tx, ry, sy, ty, rxy, sxy, ryx, syx,
+    cc, c_sib, c_sum, rx, sx, tx, ry, sy, ty, rxy, ryx,
     rest, zr2, zs2, all_z, own_right, wide, sq,
     send, recv, local,
 ):
@@ -380,19 +394,16 @@
         jnp.int32, (256, 256), 1
     )
     inv[...] = jnp.where(same, 1.0, 0.0).astype(F32)
+    for copy in gram_in:
+        copy.wait_recv()
+    factor_block(0, a, inv)
     y_first.middle()
     x_first.middle()
-    for copy in gram_in:
-        copy.wait_recv()
-
-    factor_block(0, a, inv)
+    factor_block(1, a, inv)
     tx[...] = x_first.total()
-    then_y = RingSum(links, "dp_0", ys, lambda y: tx.at[rows_at(y * 32, 32)], ryx, syx)
+    then_y = DirectSum(links, "dp_0", ys, lambda y: tx.at[rows_at(y * 32, 32)], ryx)
     ty[...] = y_first.total()
-    then_x = RingSum(links, "tensor_0", xs, lambda x: ty.at[x], rxy, sxy)
-    factor_block(1, a, inv)
-    then_y.middle()
-    then_x.middle()
+    then_x = DirectSum(links, "tensor_0", xs, lambda x: ty.at[x], rxy)
     factor_block(2, a, inv)
     rest[:32, :] = then_y.total()
     rest[32:, :] = then_x.total()
@@ -418,14 +429,13 @@
     mine = three(halves(all_z[...]), inverse, across)
     own_right[0, rows_at(me.y * 32, 32), :] = mine[:32]
     own_right[1, rows_at(me.y * 32, 32), :] = mine[32:]
-    right_y = RingSpread(
-        links, "dp_0", ys, lambda y: own_right.at[:, rows_at(y * 32, 32)]
-    )
+    own_part = own_right.at[:, rows_at(me.y * 32, 32)]
+    came = [links.to(own_part, own_part, {"dp_0": there}) for there in ys[1:]]
     ortho = three((lh[...], ll[...]), inverse, across)
     ortho_out[...] = ortho
     ob[...] = (ortho * 0.05).astype(BF16)
-    right_y.middle()
-    right_y.finish()
+    for copy in came:
+        copy.wait_recv()
     wide[index, :128, :] = own_right[0].astype(BF16)
     wide[index, 128:, :] = own_right[1].astype(BF16)
     gw = Gather(me, links, wide.at[index], lambda x, c: wide.at[2 * x + c])
@@ -449,11 +459,10 @@
 
 
 def apply_kernel(buf, ob, wide, ortho, q, new_out, ortho_out, q_out):
-    lhs = ob[...]
-    for b in range(8):
+    for b in range(2):
         cols = slice(256 * b, 256 * b + 256)
         update = lax.dot_general(
-            lhs, wide[b], (((1,), (1,)), ((), ())), preferred_element_type=F32
+            ob[...], wide[b], (((1,), (1,)), ((), ())), preferred_element_type=F32
         )
         new_out[:, cols] = buf[:, cols] - update
     ortho_out[...] = ortho[...]
@@ -461,25 +470,26 @@
 
 
 def apply_update(buf, ob, wide, ortho, q):
-    def tile(rows, cols):
-        return pl.BlockSpec((rows, cols), lambda i: (i, 0))
-
+    def rows(height):
+        return pl.BlockSpec((height, 256), lambda i: (i, 0))
+
+    cols = pl.BlockSpec((640, 512), lambda i: (0, i))
     return pl.pallas_call(
         apply_kernel,
-        grid=(8,),
+        grid=(4,),
         out_shape=(
             jax.ShapeDtypeStruct((640, 2048), F32),
             jax.ShapeDtypeStruct((640, 256), F32),
             jax.ShapeDtypeStruct((256, 256), F32),
         ),
         in_specs=[
-            tile(80, 2048),
-            tile(80, 256),
-            pl.BlockSpec((8, 256, 256), lambda i: (0, 0, 0)),
-            tile(80, 256),
-            tile(32, 256),
+            cols,
+            pl.BlockSpec((640, 256), lambda i: (0, 0)),
+            pl.BlockSpec((2, 256, 256), lambda i: (i, 0, 0)),
+            rows(160),
+            rows(64),
         ],
-        out_specs=(tile(80, 2048), tile(80, 256), tile(32, 256)),
+        out_specs=(cols, rows(160), rows(64)),
         compiler_params=pltpu.CompilerParams(vmem_limit_bytes=56 * 2**20),
         name="apply_update",
     )(buf, ob, wide, ortho, q)
@@ -529,9 +539,7 @@
         vm((4, 32, 256), F32),
         vm((4, 32, 256), F32),
         vm((3, 32, 256), F32),
-        vm((32, 256), F32),
         vm((3, 32, 256), F32),
-        vm((32, 256), F32),
         vm((64, 256), F32),
         vm((7, 8, 256), F32),
         vm((8, 256), F32),

time: 132 us -> 126 us (0.955)
  Pallas kernels: 131 us -> 125 us
    pallas_call x1, Pallas kernels: 122 us -> 118 us  [whole_step(): pl.pallas_call(step_kernel, out_shape=(jax.ShapeDtypeStruct((640, 2048),...]
    pallas_call x1, Pallas kernels: 9.24 us -> 6.87 us  [apply_update(): pl.pallas_call(apply_kernel, grid=(4,), out_shape=(jax.ShapeDtypeStruct((...]
where the time goes in v5:
time: 126 us
  Pallas kernels  125 us (99%)
    pallas_call x1, Pallas kernels, whole_step(): pl.pallas_call(step_kernel, out_shape=(jax.ShapeDtypeStruct((640, 2048),...  118 us
    pallas_call x1, Pallas kernels, apply_update(): pl.pallas_call(apply_kernel, grid=(4,), out_shape=(jax.ShapeDtypeStruct((...  6.87 us

profile of v5, /device:TPU:1, one launch (start us, length us, event | category | flops | bytes accessed | tf_op | source)
XLA Modules:
  0.0 125.6 jit_solution(16300873048424014857)
XLA Ops:
  0.6 118.1 %whole_step.1 = (f32[640,2048]{1,0:T(8,128)}, bf16[640,256]{1,0:T(8,128)(2,1)}, bf16[8,256,256]{2,1,0:T(8,128)(2,1)}, f32[640,256]{1,0:T(8,128)}, f32[256,256]{1,0:T(8,128)}) custom-call(bf16[1024,640]{1,0:T(8,128)(2,1)} %acts.1, bf16[128,2048]{1,0:T(8,128)(2,1)} %og.1, f32[640,2048]{1,0:T(8,128)} %mom.1, f32[256,256]{1,0:T(8,128)} %q.1), custom_call_target="tpu_custom_call" | custom-call | tf_op jit(solution)/shard_map/whole_step/pallas_call | solution.py:554
  118.7 6.9 %apply_update.1 = (f32[640,2048]{1,0:T(8,128)}, f32[640,256]{1,0:T(8,128)}, f32[256,256]{1,0:T(8,128)}) custom-call(f32[640,2048]{1,0:T(8,128)} %get-tuple-element.8.buf, bf16[640,256]{1,0:T(8,128)(2,1)} %get-tuple-element.9.ob, bf16[8,256,256]{2,1,0:T(8,128)(2,1)} %get-tuple-element.10.wide, f32[640,256]{1,0:T(8,128)} %get-tuple-element.11.ortho, ...), custom_call_target="tpu_custom_call" | custom-call | tf_op jit(solution)/shard_map/apply_update/pallas_call | solution.py:477

commit v6 on v5

--- a/solution.py
+++ b/solution.py
@@ -158,6 +158,33 @@
         for copy in self.copies:
             copy.wait_recv()
         return self.mine[...] + self.came[0] + self.came[1] + self.came[2]
+
+
+class HalfGathers:
+    def __init__(self, me, links, own, slot):
+        self.parts = [
+            Gather(me, links, own(p), lambda x, c, p=p: slot(x, c, p)) for p in range(2)
+        ]
+
+    def first(self):
+        for part in self.parts:
+            part.first()
+
+    def second(self):
+        for part in self.parts:
+            part.second()
+
+    def third(self):
+        for part in self.parts:
+            part.third()
+
+    def sibling(self, n):
+        for part in self.parts:
+            getattr(part, "s%d" % n).wait_recv()
+
+    def rest(self):
+        for n in range(4):
+            self.sibling(n)
 
 
 def three(a, b, dims=((1,), (0,))):
@@ -237,7 +264,12 @@
     for load in loads:
         load.start()
     greet(me)
-    gq = Gather(me, links, q, lambda x, c: qg.at[x * 2 + c])
+    gq = HalfGathers(
+        me,
+        links,
+        lambda p: q.at[pl.ds(128 * p, 128)],
+        lambda x, c, p: qg.at[x * 2 + c, pl.ds(128 * p, 128)],
+    )
     gq.first()
     gq.second()
     loads[2].wait()
@@ -260,15 +292,15 @@
     take(me.x, me.c, True)
     take(me.xm, me.c)
     take(me.xp, me.c)
-    gq.s0.wait_recv()
+    gq.sibling(0)
     take(me.x, me.sib)
     gq.third()
     take(me.xo, me.c)
-    gq.s1.wait_recv()
+    gq.sibling(1)
     take(me.xp, me.sib)
-    gq.s2.wait_recv()
+    gq.sibling(2)
     take(me.xm, me.sib)
-    gq.s3.wait_recv()
+    gq.sibling(3)
     take(me.xo, me.sib)
     yg[me.x, own_rows, :] = y_own[...]
     own_y = yg.at[me.x, own_rows]
@@ -438,7 +470,12 @@
         copy.wait_recv()
     wide[index, :128, :] = own_right[0].astype(BF16)
     wide[index, 128:, :] = own_right[1].astype(BF16)
-    gw = Gather(me, links, wide.at[index], lambda x, c: wide.at[2 * x + c])
+    gw = HalfGathers(
+        me,
+        links,
+        lambda p: wide.at[index, pl.ds(128 * p, 128)],
+        lambda x, c, p: wide.at[2 * x + c, pl.ds(128 * p, 128)],
+    )
     values = own_right[...].reshape(256, 256)
     sq[index] = jnp.broadcast_to(jnp.sum(values * values, axis=0, keepdims=True), (8, 256))
     mark = sq.at[index]
@@ -490,7 +527,7 @@
             rows(64),
         ],
         out_specs=(cols, rows(160), rows(64)),
-        compiler_params=pltpu.CompilerParams(vmem_limit_bytes=56 * 2**20),
+        compiler_params=pltpu.CompilerParams(vmem_limit_bytes=24 * 2**20),
         name="apply_update",
     )(buf, ob, wide, ortho, q)
 
@@ -554,17 +591,17 @@
     outs = pl.pallas_call(
         step_kernel,
         out_shape=(
-            jax.ShapeDtypeStruct((640, 2048), F32),
-            jax.ShapeDtypeStruct((640, 256), BF16),
-            jax.ShapeDtypeStruct((8, 256, 256), BF16),
-            jax.ShapeDtypeStruct((640, 256), F32),
-            jax.ShapeDtypeStruct((256, 256), F32),
+            pltpu.VMEM((640, 2048), F32),
+            pltpu.VMEM((640, 256), BF16),
+            pltpu.VMEM((8, 256, 256), BF16),
+            pltpu.VMEM((640, 256), F32),
+            pltpu.VMEM((256, 256), F32),
         ),
         in_specs=[in_hbm] * 4,
-        out_specs=(any_space, in_vmem, in_vmem, in_vmem, in_vmem),
+        out_specs=(in_vmem, in_vmem, in_vmem, in_vmem, in_vmem),
         scratch_shapes=scratch,
         compiler_params=pltpu.CompilerParams(
-            collective_id=0, has_side_effects=True, vmem_limit_bytes=60 * 2**20
+            collective_id=0, has_side_effects=True, vmem_limit_bytes=56 * 2**20
         ),
         name="whole_step",
     )(acts, out_grad, momentum, q_basis)

time: 126 us -> 119 us (0.944)
  Pallas kernels: 125 us -> 118 us
    pallas_call x1, Pallas kernels: 118 us -> 115 us  [whole_step(): pl.pallas_call(step_kernel, out_shape=(pltpu.VMEM((640, 2048), F32), pltp...]
    pallas_call x1, Pallas kernels: 6.87 us -> 3.68 us  [apply_update(): pl.pallas_call(apply_kernel, grid=(4,), out_shape=(jax.ShapeDtypeStruct((...]
where the time goes in v6:
time: 119 us
  Pallas kernels  118 us (99%)
    pallas_call x1, Pallas kernels, whole_step(): pl.pallas_call(step_kernel, out_shape=(pltpu.VMEM((640, 2048), F32), pltp...  115 us
    pallas_call x1, Pallas kernels, apply_update(): pl.pallas_call(apply_kernel, grid=(4,), out_shape=(jax.ShapeDtypeStruct((...  3.68 us

profile of v6, /device:TPU:1, one launch (start us, length us, event | category | flops | bytes accessed | tf_op | source)
XLA Modules:
  0.0 118.8 jit_solution(15555077795170023526)
XLA Ops:
  0.6 114.5 %whole_step.1 = (f32[640,2048]{1,0:T(8,128)S(1)}, bf16[640,256]{1,0:T(8,128)(2,1)S(1)}, bf16[8,256,256]{2,1,0:T(8,128)(2,1)S(1)}, f32[640,256]{1,0:T(8,128)S(1)}, f32[256,256]{1,0:T(8,128)S(1)}) custom-call(bf16[1024,640]{1,0:T(8,128)(2,1)} %acts.1, bf16[128,2048]{1,0:T(8,128)(2,1)} %og.1, f32[640,2048]{1,0:T(8,128)} %mom.1, f32[256,256]{1,0:T(8,128)} %q.1), custom_call_target="tpu_custom_call" | custom-call | tf_op jit(solution)/shard_map/whole_step/pallas_call | solution.py:591
  115.2 3.7 %apply_update.1 = (f32[640,2048]{1,0:T(8,128)}, f32[640,256]{1,0:T(8,128)}, f32[256,256]{1,0:T(8,128)}) custom-call(f32[640,2048]{1,0:T(8,128)S(1)} %get-tuple-element.8.buf, bf16[640,256]{1,0:T(8,128)(2,1)S(1)} %get-tuple-element.9.ob, bf16[8,256,256]{2,1,0:T(8,128)(2,1)S(1)} %get-tuple-element.10.wide, f32[640,256]{1,0:T(8,128)S(1)} %get-tuple-element.11.ortho, ...), custom_call_target="tpu_custom_call" | custom-call | tf_op jit(solution)/shard_map/apply_update/pallas_call | solution.py:514

commit v7 on v6

--- a/solution.py
+++ b/solution.py
@@ -303,8 +303,10 @@
     gq.sibling(3)
     take(me.xo, me.sib)
     yg[me.x, own_rows, :] = y_own[...]
-    own_y = yg.at[me.x, own_rows]
-    gy = Gather(me, links, own_y, lambda x, c: yg.at[x, pl.ds(pl.multiple_of(c * 128, 128), 128)])
+    def y_piece(x, c, p):
+        return yg.at[x, rows_at(c * 128 + 64 * p, 64, 64)]
+
+    gy = HalfGathers(me, links, lambda p: y_piece(me.x, me.c, p), y_piece)
 
     def momentum_part(t):
         rows = rows_at(t * 128, 128)
@@ -336,13 +338,22 @@
             piece = acc[:, 128 * half : 128 * half + 128]
             part[half, rows, :] = (0.95 * part[half, rows, :] + piece) * (1 / 32)
 
-    def of_y(ref, y):
-        return ref.at[:, pl.ds(pl.multiple_of(y * 160, 32), 160)]
-
     ys, xs = (me.y, me.yp, me.ym, me.yo), (me.x, me.xp, me.xm, me.xo)
-    ring = RingSum(links, "dp_0", ys, lambda y: of_y(part, y), r_left, s1)
-    ring.middle()
-    chunk[...] = ring.total()
+    rings = [
+        RingSum(
+            links,
+            "dp_0",
+            ys,
+            lambda y, h=h: part.at[h, rows_at(y * 160, 160, 32)],
+            r_left.at[h],
+            s1.at[h],
+        )
+        for h in range(2)
+    ]
+    for ring in rings:
+        ring.middle()
+    for h in range(2):
+        chunk[h] = rings[h].total()
 
     def z_rows(z):
         return z // 4, pl.multiple_of(lax.rem(z, 4) * 40, 8)
@@ -368,7 +379,10 @@
     go.third()
     for copy in came:
         copy.wait_recv()
-    spread = RingSpread(links, "dp_0", ys, lambda y: of_y(full, y))
+    spreads = [
+        RingSpread(links, "dp_0", ys, lambda y, h=h: full.at[h, rows_at(y * 160, 160, 32)])
+        for h in range(2)
+    ]
 
     def buffer_part(n):
         cols = rows_at(n * 256, 256, 256)
@@ -380,11 +394,13 @@
 
     go.rest()
     pl.loop(0, 4)(buffer_part)
-    spread.middle()
+    for spread in spreads:
+        spread.middle()
     pl.loop(4, 8)(buffer_part)
     store = pltpu.make_async_copy(buf, buf_out, local.at[4])
     store.start()
-    spread.finish()
+    for spread in spreads:
+        spread.finish()
     lt = []
     for half in range(2):
         cols = slice(128 * half, 128 * half + 128)
@@ -536,7 +552,7 @@
     any_space = pl.BlockSpec(memory_space=pl.ANY)
     in_hbm = pl.BlockSpec(memory_space=pltpu.HBM)
     in_vmem = pl.BlockSpec(memory_space=pltpu.VMEM)
-    copies = 120
+    copies = 140
     vm = pltpu.VMEM
     scratch = [
         vm((1024, 640), BF16),
@@ -551,7 +567,7 @@
         vm((4, 256, 2048), BF16),
         vm((128, 256), F32),
         vm((2, 640, 128), F32),
-        vm((3, 2, 160, 128), F32),
+        vm((2, 3, 160, 128), F32),
         vm((2, 160, 128), F32),
         vm((2, 160, 128), F32),
         vm((7, 40, 128), F32),

time: 119 us -> 117 us (0.983)
  Pallas kernels: 118 us -> 116 us
    pallas_call x1, Pallas kernels: 115 us -> 112 us  [whole_step(): pl.pallas_call(step_kernel, out_shape=(pltpu.VMEM((640, 2048), F32), pltp...]
where the time goes in v7:
time: 117 us
  Pallas kernels  116 us (99%)
    pallas_call x1, Pallas kernels, whole_step(): pl.pallas_call(step_kernel, out_shape=(pltpu.VMEM((640, 2048), F32), pltp...  112 us
    pallas_call x1, Pallas kernels, apply_update(): pl.pallas_call(apply_kernel, grid=(4,), out_shape=(jax.ShapeDtypeStruct((...  3.68 us

profile of v7, /device:TPU:1, one launch (start us, length us, event | category | flops | bytes accessed | tf_op | source)
XLA Modules:
  0.0 116.6 jit_solution(5975853459797270543)
XLA Ops:
  0.6 112.2 %whole_step.1 = (f32[640,2048]{1,0:T(8,128)S(1)}, bf16[640,256]{1,0:T(8,128)(2,1)S(1)}, bf16[8,256,256]{2,1,0:T(8,128)(2,1)S(1)}, f32[640,256]{1,0:T(8,128)S(1)}, f32[256,256]{1,0:T(8,128)S(1)}) custom-call(bf16[1024,640]{1,0:T(8,128)(2,1)} %acts.1, bf16[128,2048]{1,0:T(8,128)(2,1)} %og.1, f32[640,2048]{1,0:T(8,128)} %mom.1, f32[256,256]{1,0:T(8,128)} %q.1), custom_call_target="tpu_custom_call" | custom-call | tf_op jit(solution)/shard_map/whole_step/pallas_call | solution.py:607
  112.9 3.7 %apply_update.1 = (f32[640,2048]{1,0:T(8,128)}, f32[640,256]{1,0:T(8,128)}, f32[256,256]{1,0:T(8,128)}) custom-call(f32[640,2048]{1,0:T(8,128)S(1)} %get-tuple-element.8.buf, bf16[640,256]{1,0:T(8,128)(2,1)S(1)} %get-tuple-element.9.ob, bf16[8,256,256]{2,1,0:T(8,128)(2,1)S(1)} %get-tuple-element.10.wide, f32[640,256]{1,0:T(8,128)S(1)} %get-tuple-element.11.ortho, ...), custom_call_target="tpu_custom_call" | custom-call | tf_op jit(solution)/shard_map/apply_update/pallas_call | solution.py:530

commit v8 on v7

--- a/solution.py
+++ b/solution.py
@@ -161,9 +161,9 @@
 
 
 class HalfGathers:
-    def __init__(self, me, links, own, slot):
+    def __init__(self, me, links, own, slot, pieces=2):
         self.parts = [
-            Gather(me, links, own(p), lambda x, c, p=p: slot(x, c, p)) for p in range(2)
+            Gather(me, links, own(p), lambda x, c, p=p: slot(x, c, p)) for p in range(pieces)
         ]
 
     def first(self):
@@ -267,8 +267,9 @@
     gq = HalfGathers(
         me,
         links,
-        lambda p: q.at[pl.ds(128 * p, 128)],
-        lambda x, c, p: qg.at[x * 2 + c, pl.ds(128 * p, 128)],
+        lambda p: q.at[pl.ds(64 * p, 64)],
+        lambda x, c, p: qg.at[x * 2 + c, pl.ds(64 * p, 64)],
+        pieces=4,
     )
     gq.first()
     gq.second()
@@ -552,7 +553,7 @@
     any_space = pl.BlockSpec(memory_space=pl.ANY)
     in_hbm = pl.BlockSpec(memory_space=pltpu.HBM)
     in_vmem = pl.BlockSpec(memory_space=pltpu.VMEM)
-    copies = 140
+    copies = 160
     vm = pltpu.VMEM
     scratch = [
         vm((1024, 640), BF16),

time: 117 us -> 117 us (level)
  no operation moved by 1% of the time
where the time goes in v8:
time: 117 us; the launch traced here: 116 us
  Pallas kernels  116 us (99%)
    pallas_call x1, Pallas kernels, whole_step(): pl.pallas_call(step_kernel, out_shape=(pltpu.VMEM((640, 2048), F32), pltp...  112 us
    pallas_call x1, Pallas kernels, apply_update(): pl.pallas_call(apply_kernel, grid=(4,), out_shape=(jax.ShapeDtypeStruct((...  3.68 us

profile of v8, /device:TPU:1, one launch (start us, length us, event | category | flops | bytes accessed | tf_op | source)
XLA Modules:
  0.0 116.4 jit_solution(6377833558882963037)
XLA Ops:
  0.6 112.1 %whole_step.1 = (f32[640,2048]{1,0:T(8,128)S(1)}, bf16[640,256]{1,0:T(8,128)(2,1)S(1)}, bf16[8,256,256]{2,1,0:T(8,128)(2,1)S(1)}, f32[640,256]{1,0:T(8,128)S(1)}, f32[256,256]{1,0:T(8,128)S(1)}) custom-call(bf16[1024,640]{1,0:T(8,128)(2,1)} %acts.1, bf16[128,2048]{1,0:T(8,128)(2,1)} %og.1, f32[640,2048]{1,0:T(8,128)} %mom.1, f32[256,256]{1,0:T(8,128)} %q.1), custom_call_target="tpu_custom_call" | custom-call | tf_op jit(solution)/shard_map/whole_step/pallas_call | solution.py:608
  112.8 3.7 %apply_update.1 = (f32[640,2048]{1,0:T(8,128)}, f32[640,256]{1,0:T(8,128)}, f32[256,256]{1,0:T(8,128)}) custom-call(f32[640,2048]{1,0:T(8,128)S(1)} %get-tuple-element.8.buf, bf16[640,256]{1,0:T(8,128)(2,1)S(1)} %get-tuple-element.9.ob, bf16[8,256,256]{2,1,0:T(8,128)(2,1)S(1)} %get-tuple-element.10.wide, f32[640,256]{1,0:T(8,128)S(1)} %get-tuple-element.11.ortho, ...), custom_call_target="tpu_custom_call" | custom-call | tf_op jit(solution)/shard_map/apply_update/pallas_call | solution.py:531
